TPU v7x, 32 devices: a whole 2x2x4 slice. The times are simulated.
32 devices in a mesh: seq: 16 (over z, y, core), head: 2 (over x).
Axes of the slice: x: 2, y: 2, z: 4, core: 2. Of those that a mesh axis runs over, the one named last changes fastest.
Arguments:
- noisy_q: bfloat16 [4160, 3072], P('seq', 'head'), may hold values from -38 to 38
- noisy_k: bfloat16 [4160, 1024], P('seq', 'head'), may hold values from -38 to 38
- noisy_value: bfloat16 [4160, 1024], P('seq', 'head'), may hold values from -6 to 6
- clean_k: bfloat16 [4160, 1024], P('seq', 'head'), may hold values from -38 to 38
- clean_value: bfloat16 [4160, 1024], P('seq', 'head'), may hold values from -6 to 6
- q_gain: float32 [3072], P('head'), may hold values from 0.1 to 1.9
- key_norm_gain: float32 [1024], P('head'), may hold values from 0.1 to 1.9
- out_grad: bfloat16 [4160, 3072], P('seq', 'head'), may hold values from -18 to 18
- window: int32 [8, 2], replicated, may hold values from -1 to 6, as said below
Outputs:
- attn_out: bfloat16 [4160, 3072], P('seq', 'head')
- grad_q: bfloat16 [4160, 3072], P('seq', 'head')
- grad_k: bfloat16 [4160, 1024], P('seq', 'head')
- grad_v: bfloat16 [4160, 1024], P('seq', 'head')
- grad_clean_k: bfloat16 [4160, 1024], P('seq', 'head')
- grad_clean_v: bfloat16 [4160, 1024], P('seq', 'head')
Inputs may be any that keep to these rules, and one draw needn't show every extreme that they name: `window`: row c lists, in an order drawn from the seed, the clean stretch c - 1 and one clean stretch from c - 3 to c - 2 that is 0 or later; an entry is -1 where no such stretch exists.
All inputs are finite; a program needn't handle non-finite values.
Results may differ from a plain program's by a relative error of at most 0.04.
Values may be sent and summed in bfloat16 or wider, within the bound.
A program may use at most 64 MiB of HBM per device.

v0:
```python
import jax
import jax.numpy as jnp
from jax import lax
from jax.sharding import PartitionSpec as P

HEAD_SIZE = 128
KEY_VALUE_HEADS = 8
GROUP = 3
STRETCH = 520
WINDOW = 3
SLOTS = 2
HQ = 24


EPSILON = 1e-06
NEG_FILL = -1e30


def shifted(value, axis, steps):
    count = lax.axis_size(axis)
    initial, last = (max(0, -steps), min(count, count - steps))
    return lax.ppermute(value, axis, [(source, source + steps) for source in range(initial, last)])


def as_sent(array):
    return jax.tree.map(lambda a: a.astype(jnp.bfloat16) if a.dtype == jnp.float32 else a, array)


def assemble(pieces, slot_pos, stretch_span):
    stacked = jnp.stack(pieces[::-1], axis=0)
    taken = lax.dynamic_slice_in_dim(stacked, stretch_span - 1 - slot_pos, stretch_span, 0)
    return taken.reshape(stretch_span * pieces[0].shape[0], pieces[0].shape[1])


def attend(q_norm, out_grad, every_key, key_mask, local_kv):
    rows_dev = q_norm.shape[0]
    score_scale = HEAD_SIZE ** (-0.5)
    per_block = next(
        (count for count in range(1, GROUP + 1) if GROUP % count == 0 and count * rows_dev >= 512),
        GROUP,
    )
    out_parts, dq_parts, dk_parts, dv_parts = ([], [], [], [])
    for key_value_head in range(local_kv):
        key_cols = every_key[:, key_value_head * HEAD_SIZE : (key_value_head + 1) * HEAD_SIZE]
        value_columns = every_key[
            :, (local_kv + key_value_head) * HEAD_SIZE : (local_kv + key_value_head + 1) * HEAD_SIZE
        ]
        dk_total = jnp.zeros((every_key.shape[0], HEAD_SIZE), dtype=jnp.float32)
        dv_total = jnp.zeros((every_key.shape[0], HEAD_SIZE), dtype=jnp.float32)
        for block_tile in range(GROUP // per_block):
            first_col = (key_value_head * GROUP + block_tile * per_block) * HEAD_SIZE
            last_col = first_col + per_block * HEAD_SIZE
            query_rows = q_norm[:, first_col:last_col].reshape(rows_dev * per_block, HEAD_SIZE)
            out_grads = out_grad[:, first_col:last_col].reshape(rows_dev * per_block, HEAD_SIZE)
            scores = (
                lax.dot_general(
                    query_rows,
                    key_cols,
                    (((1,), (1,)), ((), ())),
                    preferred_element_type=jnp.float32,
                )
                * score_scale
            )
            scores = jnp.where(key_mask[None, :], scores, NEG_FILL)
            row_max = jnp.max(scores, axis=1, keepdims=True)
            weights = jnp.exp(scores - row_max)
            probs = weights / jnp.sum(weights, axis=1, keepdims=True)
            probs_low = probs.astype(jnp.bfloat16)
            head_out = jnp.dot(probs_low, value_columns, preferred_element_type=jnp.float32)
            out_parts.append(head_out.astype(jnp.bfloat16).reshape(rows_dev, per_block * HEAD_SIZE))
            dprobs = lax.dot_general(
                out_grads,
                value_columns,
                (((1,), (1,)), ((), ())),
                preferred_element_type=jnp.float32,
            )
            row_delta = jnp.sum(out_grads.astype(jnp.float32) * head_out, axis=1, keepdims=True)
            dscores = (probs * (dprobs - row_delta) * score_scale).astype(jnp.bfloat16)
            dq_parts.append(
                jnp.dot(dscores, key_cols, preferred_element_type=jnp.float32).reshape(
                    rows_dev, per_block * HEAD_SIZE
                )
            )
            dk_total = dk_total + lax.dot_general(
                dscores, query_rows, (((0,), (0,)), ((), ())), preferred_element_type=jnp.float32
            )
            dv_total = dv_total + lax.dot_general(
                probs_low, out_grads, (((0,), (0,)), ((), ())), preferred_element_type=jnp.float32
            )
        dk_parts.append(dk_total)
        dv_parts.append(dv_total)
    return (
        jnp.concatenate(out_parts, axis=1),
        jnp.concatenate(dq_parts, axis=1),
        jnp.concatenate(dk_parts + dv_parts, axis=1),
    )


def on_device(
    noisy_q, noisy_k, noisy_value, clean_k, clean_value, q_gain, key_norm_gain, out_grad, window
):
    rows_dev = noisy_q.shape[0]
    local_kv = noisy_k.shape[1] // HEAD_SIZE
    stretch_span = STRETCH // rows_dev
    seq_pos = lax.axis_index("seq")
    stretch_id = seq_pos // stretch_span
    slot_pos = seq_pos % stretch_span
    q_full = noisy_q.astype(jnp.float32)
    k_full = noisy_k.astype(jnp.float32)
    c_full = clean_k.astype(jnp.float32)
    totals = lax.psum(
        (
            jnp.sum(q_full * q_full, axis=1),
            jnp.sum(k_full * k_full, axis=1),
            jnp.sum(c_full * c_full, axis=1),
        ),
        "head",
    )
    q_width = HQ * HEAD_SIZE
    key_width = KEY_VALUE_HEADS * HEAD_SIZE
    q_inv = lax.rsqrt(totals[0] / q_width + EPSILON)[:, None]
    k_inv = lax.rsqrt(totals[1] / key_width + EPSILON)[:, None]
    c_inv = lax.rsqrt(totals[2] / key_width + EPSILON)[:, None]
    q_norm = (q_full * q_inv * q_gain[None, :]).astype(jnp.bfloat16)
    k_norm = (k_full * k_inv * key_norm_gain[None, :]).astype(jnp.bfloat16)
    c_norm = (c_full * c_inv * key_norm_gain[None, :]).astype(jnp.bfloat16)
    noisy_kv = jnp.concatenate([k_norm, noisy_value], axis=1)
    clean_kv = jnp.concatenate([c_norm, clean_value], axis=1)
    kv_width = noisy_kv.shape[1]
    offsets = list(range(1 - stretch_span, stretch_span))
    pair_list = []
    for shift_by in offsets:
        if shift_by == 0:
            pair_list.append((noisy_kv, clean_kv))
        else:
            pair_list.append(shifted((noisy_kv, clean_kv), "seq", shift_by))
    noisy_whole = assemble([item[0] for item in pair_list], slot_pos, stretch_span)
    clean_whole = assemble([item[1] for item in pair_list], slot_pos, stretch_span)
    earlier = []
    for back_by in range(WINDOW, 0, -1):
        earlier.append(shifted(clean_whole, "seq", stretch_span * back_by))
    clean_all = jnp.concatenate(earlier, axis=0)
    row_hit = jnp.arange(window.shape[0], dtype=jnp.int32)[:, None] == stretch_id
    listed = jnp.sum(jnp.where(row_hit, window, 0), axis=0)
    first_stretch = stretch_id - WINDOW
    blocks = [noisy_whole]
    mask_parts = [jnp.ones((STRETCH,), dtype=bool)]
    flags = []
    places = []
    for j in range(SLOTS):
        is_listed = listed[j] >= 0
        place_at = jnp.clip(listed[j] - first_stretch, 0, WINDOW - 1)
        blocks.append(lax.dynamic_slice_in_dim(clean_all, place_at * STRETCH, STRETCH, 0))
        mask_parts.append(jnp.broadcast_to(is_listed, (STRETCH,)))
        flags.append(is_listed)
        places.append(place_at)
    attn_out, dq_norm, dkv_all = attend(
        q_norm,
        out_grad,
        jnp.concatenate(blocks, axis=0),
        jnp.concatenate(mask_parts, axis=0),
        local_kv,
    )
    noisy_grad = dkv_all[:STRETCH]
    clean_grad = []
    for place_idx in range(WINDOW):
        summed = jnp.zeros((STRETCH, kv_width), dtype=jnp.float32)
        for j in range(SLOTS):
            summed = summed + jnp.where(
                flags[j] & (places[j] == place_idx),
                dkv_all[(1 + j) * STRETCH : (2 + j) * STRETCH],
                0.0,
            )
        clean_grad.append(summed)
    noisy_total = lax.dynamic_slice_in_dim(noisy_grad, slot_pos * rows_dev, rows_dev, 0)
    clean_own = jnp.zeros((STRETCH, kv_width), dtype=jnp.float32)
    for back_by in range(1, WINDOW + 1):
        clean_own = clean_own + shifted(
            as_sent(clean_grad[WINDOW - back_by]), "seq", -stretch_span * back_by
        )
    clean_total = lax.dynamic_slice_in_dim(clean_own, slot_pos * rows_dev, rows_dev, 0)
    for shift_by in offsets:
        if shift_by != 0:
            send_row = jnp.clip(slot_pos + shift_by, 0, stretch_span - 1) * rows_dev
            received = shifted(
                (
                    as_sent(lax.dynamic_slice_in_dim(noisy_grad, send_row, rows_dev, 0)),
                    as_sent(lax.dynamic_slice_in_dim(clean_own, send_row, rows_dev, 0)),
                ),
                "seq",
                shift_by,
            )
            inside = (slot_pos - shift_by >= 0) & (slot_pos - shift_by < stretch_span)
            noisy_total = noisy_total + jnp.where(inside, received[0], 0.0)
            clean_total = clean_total + jnp.where(inside, received[1], 0.0)
    key_columns = local_kv * HEAD_SIZE
    q_scaled = dq_norm * q_gain[None, :]
    k_scaled = noisy_total[:, :key_columns] * key_norm_gain[None, :]
    c_scaled = clean_total[:, :key_columns] * key_norm_gain[None, :]
    inner_sum = lax.psum(
        (
            jnp.sum(q_scaled * q_full, axis=1),
            jnp.sum(k_scaled * k_full, axis=1),
            jnp.sum(c_scaled * c_full, axis=1),
        ),
        "head",
    )
    grad_q = (
        q_inv * q_scaled - q_full * q_inv * q_inv * q_inv * (inner_sum[0] / q_width)[:, None]
    ).astype(jnp.bfloat16)
    grad_k = (
        k_inv * k_scaled - k_full * k_inv * k_inv * k_inv * (inner_sum[1] / key_width)[:, None]
    ).astype(jnp.bfloat16)
    grad_clean_k = (
        c_inv * c_scaled - c_full * c_inv * c_inv * c_inv * (inner_sum[2] / key_width)[:, None]
    ).astype(jnp.bfloat16)
    grad_v = noisy_total[:, key_columns:].astype(jnp.bfloat16)
    grad_clean_v = clean_total[:, key_columns:].astype(jnp.bfloat16)
    return (attn_out, grad_q, grad_k, grad_v, grad_clean_k, grad_clean_v)


def solution(mesh):
    placed = (
        P("seq", "head"),
        P("seq", "head"),
        P("seq", "head"),
        P("seq", "head"),
        P("seq", "head"),
        P("head"),
        P("head"),
        P("seq", "head"),
        P(),
    )
    return jax.shard_map(
        on_device,
        mesh=mesh,
        in_specs=placed,
        out_specs=(
            P("seq", "head"),
            P("seq", "head"),
            P("seq", "head"),
            P("seq", "head"),
            P("seq", "head"),
            P("seq", "head"),
        ),
        check_vma=False,
    )
```

profile of v0, /device:TPU:14, one launch (start us, length us, event | category | flops | bytes accessed | tf_op | source)
XLA Modules:
  0.0 325.9 jit_solution(18347567622818572351)
XLA Ops:
  4.3 5.0 %all-reduce.1 = (f32[260]{0:T(512)S(1)}, f32[260]{0:T(512)S(1)}, f32[260]{0:T(512)S(1)}) all-reduce(f32[260]{0:T(512)S(1)} %fusion.27, f32[260]{0:T(512)S(1)} %fusion.61, f32[260]{0:T(512)S(1)} %fusion.59), channel_id=1, replica_groups=mesh['seq'=16,'head'=2] {'head'}, use_global_device_ids=true, to_apply=%region_2.3 | all-reduce | flops 780 | bytes 6240 | tf_op jit(solution)/shard_map/psum | solution.py:111
  14.4 3.6 %collective-permute-start.3 = (bf16[260,1024]{1,0:T(8,128)(2,1)}, bf16[260,1024]{1,0:T(8,128)(2,1)}, u32[]{:S(2)}, u32[]{:S(2)}) collective-permute-start(bf16[260,1024]{1,0:T(8,128)(2,1)} %get-tuple-element.42), channel_id=1, source_target_pairs={{2,0},{4,2},{6,4},{8,6},{10,8},{12,10},{14,12},{16,14},{18,16},{20... | collective-permute-start | bytes 1597448 | tf_op jit(solution)/shard_map/ppermute | solution.py:22
  20.8 3.6 %collective-permute-start.1 = (bf16[260,1024]{1,0:T(8,128)(2,1)}, bf16[260,1024]{1,0:T(8,128)(2,1)}, u32[]{:S(2)}, u32[]{:S(2)}) collective-permute-start(bf16[260,1024]{1,0:T(8,128)(2,1)} %get-tuple-element.40), channel_id=1, source_target_pairs={{2,0},{4,2},{6,4},{8,6},{10,8},{12,10},{14,12},{16,14},{18,16},{20... | collective-permute-start | bytes 1597448 | tf_op jit(solution)/shard_map/ppermute | solution.py:22
  25.4 3.8 %collective-permute-done.2 = bf16[260,1024]{1,0:T(8,128)(2,1)} collective-permute-done((bf16[260,1024]{1,0:T(8,128)(2,1)}, bf16[260,1024]{1,0:T(8,128)(2,1)}, u32[]{:S(2)}, u32[]{:S(2)}) %collective-permute-start.2) | collective-permute-done | bytes 532512 | tf_op jit(solution)/shard_map/ppermute | solution.py:22
  29.2 4.7 %collective-permute-done.3 = bf16[260,1024]{1,0:T(8,128)(2,1)} collective-permute-done((bf16[260,1024]{1,0:T(8,128)(2,1)}, bf16[260,1024]{1,0:T(8,128)(2,1)}, u32[]{:S(2)}, u32[]{:S(2)}) %collective-permute-start.3) | collective-permute-done | bytes 532512 | tf_op jit(solution)/shard_map/ppermute | solution.py:22
  39.0 2.8 collective-permute-start.5
  46.1 5.0 %collective-permute-start.6 = (bf16[520,1024]{1,0:T(8,128)(2,1)}, bf16[520,1024]{1,0:T(8,128)(2,1)}, u32[]{:S(2)}, u32[]{:S(2)}) collective-permute-start(bf16[520,1024]{1,0:T(8,128)(2,1)} %reshape.94), channel_id=1, source_target_pairs={{0,4},{2,6},{4,8},{6,10},{8,12},{10,14},{12,16},{14,18},{16,20},{1... | collective-permute-start | bytes 3194888 | tf_op jit(solution)/shard_map/ppermute | solution.py:22
  57.1 10.1 %collective-permute-done = bf16[260,1024]{1,0:T(8,128)(2,1)} collective-permute-done((bf16[260,1024]{1,0:T(8,128)(2,1)}, bf16[260,1024]{1,0:T(8,128)(2,1)}, u32[]{:S(2)}, u32[]{:S(2)}) %collective-permute-start) | collective-permute-done | bytes 532512 | tf_op jit(solution)/shard_map/ppermute | solution.py:22
  70.1 11.4 %collective-permute-done.4 = bf16[520,1024]{1,0:T(8,128)(2,1)} collective-permute-done((bf16[520,1024]{1,0:T(8,128)(2,1)}, bf16[520,1024]{1,0:T(8,128)(2,1)}, u32[]{:S(2)}, u32[]{:S(2)}) %collective-permute-start.4) | collective-permute-done | bytes 1064992 | tf_op jit(solution)/shard_map/ppermute | solution.py:22
  82.9 21.5 %collective-permute-done.5 = bf16[520,1024]{1,0:T(8,128)(2,1)} collective-permute-done((bf16[520,1024]{1,0:T(8,128)(2,1)}, bf16[520,1024]{1,0:T(8,128)(2,1)}, u32[]{:S(2)}, u32[]{:S(2)}) %collective-permute-start.5) | collective-permute-done | bytes 1064992 | tf_op jit(solution)/shard_map/ppermute | solution.py:22
  105.7 21.5 %collective-permute-done.6 = bf16[520,1024]{1,0:T(8,128)(2,1)} collective-permute-done((bf16[520,1024]{1,0:T(8,128)(2,1)}, bf16[520,1024]{1,0:T(8,128)(2,1)}, u32[]{:S(2)}, u32[]{:S(2)}) %collective-permute-start.6) | collective-permute-done | bytes 1064992 | tf_op jit(solution)/shard_map/ppermute | solution.py:22
  132.8 5.5 %fusion.13 = (f32[780]{0:T(1024)S(1)}, f32[780]{0:T(1024)S(1)}, f32[780]{0:T(1024)S(1)}, f32[780]{0:T(1024)S(1)}, f32[780,1560]{1,0:T(8,128)}) fusion(f32[780,1560]{1,0:T(8,128)S(1)} %get-tuple-element.62, f32[780]{0:T(1024)S(1)} %get-tuple-element.61, pred[1560]{0:T(1024)(128)(4,1)S(1)} %concatenate.24, f32[780,1560]{1,0:T(8,128)S(1)} %fusion.73, ...), kind=kOutput, calls=%fused_computation.25 | convolution fusion | flops 327316128 | bytes 21140800 | tf_op jit(solution)/shard_map/dot_general | solution.py:56
  138.3 8.7 %fusion.15 = (f32[780]{0:T(1024)S(1)}, f32[780]{0:T(1024)S(1)}, f32[780]{0:T(1024)S(1)}, f32[780,1560]{1,0:T(8,128)}) fusion(f32[780,1560]{1,0:T(8,128)} %get-tuple-element.63, f32[780]{0:T(1024)S(1)} %get-tuple-element.9, pred[1560]{0:T(1024)(128)(4,1)S(1)} %concatenate.24, f32[780]{0:T(1024)S(1)} %get-tuple-element.10, f32[780,1560]{1,0:T(8,128)S(1)} %fusion.73, ...), kind=kLoop, calls=%fused_computation.27 | loop fusion | flops 19466460 | bytes 24362520 | tf_op jit(solution)/shard_map/reduce_sum | solution.py:67
  147.0 8.6 %fusion.14 = (f32[780,1560]{1,0:T(8,128)}, f32[780,1560]{1,0:T(8,128)}, f32[780,1560]{1,0:T(8,128)S(1)}) fusion(f32[780,1560]{1,0:T(8,128)} %get-tuple-element.63, f32[780]{0:T(1024)S(1)} %get-tuple-element.12, f32[780]{0:T(1024)S(1)} %get-tuple-element.9, pred[1560]{0:T(1024)(128)(4,1)S(1)} %concatenate.24, f32[780]{0:T(1024)S(1)} %get-tuple-element.13, ...), kind=kLoop, calls=%fused_computation.26 | loop fusion | flops 14601600 | bytes 29223480 | tf_op jit(solution)/shard_map/div | solution.py:67
  155.6 2.2 multiply_reduce_fusion
  163.8 4.2 %multiply_reduce_fusion.1 = (f32[780]{0:T(1024)S(1)}, bf16[780,128]{1,0:T(8,128)(2,1)}) fusion(bf16[780,128]{1,0:T(8,128)(2,1)} %reshape.106, bf16[1560,1024]{1,0:T(8,128)(2,1)S(1)} %pad_maximum_fusion, f32[780,1560]{1,0:T(8,128)} %get-tuple-element.55), kind=kOutput, calls=%fused_computation.118 | convolution fusion | flops 313116192 | bytes 5669040 | tf_op jit(solution)/shard_map/dot_general | solution.py:69
  168.1 3.5 %fusion.3 = bf16[780,1560]{1,0:T(8,128)(2,1)S(1)} fusion(f32[780,1560]{1,0:T(8,128)} %get-tuple-element.55, bf16[780,128]{1,0:T(8,128)(2,1)S(1)} %copy-done.19, f32[780]{0:T(1024)S(1)} %get-tuple-element.47, bf16[1560,1024]{1,0:T(8,128)(2,1)S(1)} %pad_maximum_fusion), kind=kOutput, calls=%fused_computation.5 | convolution fusion | flops 316368000 | bytes 7904960 | tf_op jit(solution)/shard_map/dot_general | solution.py:71
  175.3 2.6 multiply_reduce_fusion.3
  189.8 3.2 fusion.89
  198.8 2.6 fusion.71
  202.5 2.8 fusion.77
  207.2 2.8 fusion.83
  212.2 2.1 collective-permute-start.8
  214.4 3.6 %collective-permute-start.7 = (bf16[260,1024]{1,0:T(8,128)(2,1)}, bf16[260,1024]{1,0:T(8,128)(2,1)}, u32[]{:S(2)}, u32[]{:S(2)}) collective-permute-start(bf16[260,1024]{1,0:T(8,128)(2,1)} %get-tuple-element.27), channel_id=1, source_target_pairs={{2,0},{4,2},{6,4},{8,6},{10,8},{12,10},{14,12},{16,14},{18,16},{20... | collective-permute-start | bytes 1597448 | tf_op jit(solution)/shard_map/ppermute | solution.py:22
  217.9 5.5 %collective-permute-done.11 = bf16[520,1024]{1,0:T(8,128)(2,1)} collective-permute-done((bf16[520,1024]{1,0:T(8,128)(2,1)}, bf16[520,1024]{1,0:T(8,128)(2,1)}, u32[]{:S(2)}, u32[]{:S(2)}) %collective-permute-start.11) | collective-permute-done | bytes 1064992 | tf_op jit(solution)/shard_map/ppermute | solution.py:22
  223.4 18.1 %collective-permute-done.10 = bf16[520,1024]{1,0:T(8,128)(2,1)} collective-permute-done((bf16[520,1024]{1,0:T(8,128)(2,1)}, bf16[520,1024]{1,0:T(8,128)(2,1)}, u32[]{:S(2)}, u32[]{:S(2)}) %collective-permute-start.10) | collective-permute-done | bytes 1064992 | tf_op jit(solution)/shard_map/ppermute | solution.py:22
  241.5 49.3 %collective-permute-done.9 = bf16[520,1024]{1,0:T(8,128)(2,1)} collective-permute-done((bf16[520,1024]{1,0:T(8,128)(2,1)}, bf16[520,1024]{1,0:T(8,128)(2,1)}, u32[]{:S(2)}, u32[]{:S(2)}) %collective-permute-start.9) | collective-permute-done | bytes 1064992 | tf_op jit(solution)/shard_map/ppermute | solution.py:22
  290.9 2.5 convert_add_fusion
  297.9 3.6 %collective-permute-start.12 = (bf16[260,1024]{1,0:T(8,128)(2,1)}, bf16[260,1024]{1,0:T(8,128)(2,1)}, u32[]{:S(2)}, u32[]{:S(2)}) collective-permute-start(bf16[260,1024]{1,0:T(8,128)(2,1)} %get-tuple-element.29), channel_id=1, source_target_pairs={{2,0},{4,2},{6,4},{8,6},{10,8},{12,10},{14,12},{16,14},{18,16},{20... | collective-permute-start | bytes 1597448 | tf_op jit(solution)/shard_map/ppermute | solution.py:22
  310.7 2.1 collective-permute-done.13
  315.2 5.6 %all-reduce = (f32[260]{0:T(512)}, f32[260]{0:T(512)S(1)}, f32[260]{0:T(512)}) all-reduce(f32[260]{0:T(512)S(1)} %copy-done.44, f32[260]{0:T(512)S(1)} %get-tuple-element.7, f32[260]{0:T(512)S(1)} %get-tuple-element.6), channel_id=1, replica_groups=mesh['seq'=16,'head'=2] {'head'}, use_global_device_ids=true, to_apply=%region_20.21 | all-reduce | flops 780 | bytes 6240 | tf_op jit(solution)/shard_map/psum | solution.py:200
  321.5 2.8 fusion.26
  (197 shorter events, 86.1 us)
Async XLA Ops:
  0.6 17.4 %copy-start.34 = (bf16[260,512]{1,0:T(8,128)(2,1)S(1)}, bf16[260,512]{1,0:T(8,128)(2,1)}, u32[]{:S(2)}) copy-start(bf16[260,512]{1,0:T(8,128)(2,1)} %param.11) | copy-start | bytes 798724
  0.6 23.9 %copy-start.30 = (bf16[260,1536]{1,0:T(8,128)(2,1)S(1)}, bf16[260,1536]{1,0:T(8,128)(2,1)}, u32[]{:S(2)}) copy-start(bf16[260,1536]{1,0:T(8,128)(2,1)} %param.16) | copy-start | bytes 2396164
  12.5 16.8 %collective-permute-start.2 = (bf16[260,1024]{1,0:T(8,128)(2,1)}, bf16[260,1024]{1,0:T(8,128)(2,1)}, u32[]{:S(2)}, u32[]{:S(2)}) collective-permute-start(bf16[260,1024]{1,0:T(8,128)(2,1)} %get-tuple-element.42), channel_id=1, source_target_pairs={{0,2},{2,4},{4,6},{6,8},{8,10},{10,12},{12,14},{14,16},{16,18},{18... | collective-permute-start | bytes 1597448 | tf_op jit(solution)/shard_map/ppermute | solution.py:22
  14.4 19.6 %collective-permute-start.3 = (bf16[260,1024]{1,0:T(8,128)(2,1)}, bf16[260,1024]{1,0:T(8,128)(2,1)}, u32[]{:S(2)}, u32[]{:S(2)}) collective-permute-start(bf16[260,1024]{1,0:T(8,128)(2,1)} %get-tuple-element.42), channel_id=1, source_target_pairs={{2,0},{4,2},{6,4},{8,6},{10,8},{12,10},{14,12},{16,14},{18,16},{20... | collective-permute-start | bytes 1597448 | tf_op jit(solution)/shard_map/ppermute | solution.py:22
  18.9 48.3 %collective-permute-start = (bf16[260,1024]{1,0:T(8,128)(2,1)}, bf16[260,1024]{1,0:T(8,128)(2,1)}, u32[]{:S(2)}, u32[]{:S(2)}) collective-permute-start(bf16[260,1024]{1,0:T(8,128)(2,1)} %get-tuple-element.40), channel_id=1, source_target_pairs={{0,2},{2,4},{4,6},{6,8},{8,10},{10,12},{12,14},{14,16},{16,18},{18... | collective-permute-start | bytes 1597448 | tf_op jit(solution)/shard_map/ppermute | solution.py:22
  20.8 46.4 %collective-permute-start.1 = (bf16[260,1024]{1,0:T(8,128)(2,1)}, bf16[260,1024]{1,0:T(8,128)(2,1)}, u32[]{:S(2)}, u32[]{:S(2)}) collective-permute-start(bf16[260,1024]{1,0:T(8,128)(2,1)} %get-tuple-element.40), channel_id=1, source_target_pairs={{2,0},{4,2},{6,4},{8,6},{10,8},{12,10},{14,12},{16,14},{18,16},{20... | collective-permute-start | bytes 1597448 | tf_op jit(solution)/shard_map/ppermute | solution.py:22
  24.6 26.6 %copy-start.38 = (f32[260]{0:T(512)}, f32[260]{0:T(512)S(1)}, u32[]{:S(2)}) copy-start(f32[260]{0:T(512)S(1)} %add_rsqrt_fusion.2) | copy-start | bytes 3124
  24.6 14.3 %copy-start.46 = (s32[8,2]{0,1:T(2,128)S(1)}, s32[8,2]{0,1:T(2,128)}, u32[]{:S(2)}) copy-start(s32[8,2]{0,1:T(2,128)} %param.17) | copy-start | bytes 196
  24.6 26.6 %copy-start.5 = (bf16[260,1536]{1,0:T(8,128)(2,1)S(1)}, bf16[260,1536]{1,0:T(8,128)(2,1)}, u32[]{:S(2)}) copy-start(bf16[260,1536]{1,0:T(8,128)(2,1)} %param.9) | copy-start | bytes 2396164
  24.6 26.6 %copy-start.35 = (f32[1536]{0:T(1024)S(1)}, f32[1536]{0:T(1024)}, u32[]{:S(2)}) copy-start(f32[1536]{0:T(1024)} %param.14) | copy-start | bytes 18436
  36.8 17.8 %copy-start.29 = (bf16[260,384]{1,0:T(8,128)(2,1)S(1)}, bf16[260,384]{1,0:T(8,128)(2,1)}, u32[]{:S(2)}) copy-start(bf16[260,384]{1,0:T(8,128)(2,1)} %get-tuple-element.34) | copy-start | bytes 599044
  36.8 18.6 %copy-start.28 = (bf16[260,384]{1,0:T(8,128)(2,1)S(1)}, bf16[260,384]{1,0:T(8,128)(2,1)}, u32[]{:S(2)}) copy-start(bf16[260,384]{1,0:T(8,128)(2,1)} %get-tuple-element.32) | copy-start | bytes 599044
  36.8 44.7 %collective-permute-start.4 = (bf16[520,1024]{1,0:T(8,128)(2,1)}, bf16[520,1024]{1,0:T(8,128)(2,1)}, u32[]{:S(2)}, u32[]{:S(2)}) collective-permute-start(bf16[520,1024]{1,0:T(8,128)(2,1)} %reshape.94), channel_id=1, source_target_pairs={{0,12},{2,14},{4,16},{6,18},{8,20},{10,22},{12,24},{14,26},{16,28}... | collective-permute-start | bytes 3194888 | tf_op jit(solution)/shard_map/ppermute | solution.py:22
  39.0 65.4 %collective-permute-start.5 = (bf16[520,1024]{1,0:T(8,128)(2,1)}, bf16[520,1024]{1,0:T(8,128)(2,1)}, u32[]{:S(2)}, u32[]{:S(2)}) collective-permute-start(bf16[520,1024]{1,0:T(8,128)(2,1)} %reshape.94), channel_id=1, source_target_pairs={{0,8},{2,10},{4,12},{6,14},{8,16},{10,18},{12,20},{14,22},{16,24},... | collective-permute-start | bytes 3194888 | tf_op jit(solution)/shard_map/ppermute | solution.py:22
  46.1 81.1 %collective-permute-start.6 = (bf16[520,1024]{1,0:T(8,128)(2,1)}, bf16[520,1024]{1,0:T(8,128)(2,1)}, u32[]{:S(2)}, u32[]{:S(2)}) collective-permute-start(bf16[520,1024]{1,0:T(8,128)(2,1)} %reshape.94), channel_id=1, source_target_pairs={{0,4},{2,6},{4,8},{6,10},{8,12},{10,14},{12,16},{14,18},{16,20},{1... | collective-permute-start | bytes 3194888 | tf_op jit(solution)/shard_map/ppermute | solution.py:22
  105.7 23.0 %copy-start.14 = (bf16[520,1024]{1,0:T(8,128)(2,1)S(1)}, bf16[520,1024]{1,0:T(8,128)(2,1)}, u32[]{:S(2)}) copy-start(bf16[520,1024]{1,0:T(8,128)(2,1)} %reshape.93) | copy-start | bytes 3194884
  129.6 41.9 %copy-start.4 = (bf16[1560,1024]{1,0:T(8,128)(2,1)}, bf16[1560,1024]{1,0:T(8,128)(2,1)S(1)}, u32[]{:S(2)}) copy-start(bf16[1560,1024]{1,0:T(8,128)(2,1)S(1)} %pad_maximum_fusion) | copy-start | bytes 9584644
  193.0 30.4 %collective-permute-start.11 = (bf16[520,1024]{1,0:T(8,128)(2,1)}, bf16[520,1024]{1,0:T(8,128)(2,1)}, u32[]{:S(2)}, u32[]{:S(2)}) collective-permute-start(bf16[520,1024]{1,0:T(8,128)(2,1)} %get-tuple-element.22), channel_id=1, source_target_pairs={{12,0},{14,2},{16,4},{18,6},{20,8},{22,10},{24,12},{26,14},{28,16}... | collective-permute-start | bytes 3194888 | tf_op jit(solution)/shard_map/ppermute | solution.py:22
  194.9 46.6 %collective-permute-start.10 = (bf16[520,1024]{1,0:T(8,128)(2,1)}, bf16[520,1024]{1,0:T(8,128)(2,1)}, u32[]{:S(2)}, u32[]{:S(2)}) collective-permute-start(bf16[520,1024]{1,0:T(8,128)(2,1)} %get-tuple-element.24), channel_id=1, source_target_pairs={{8,0},{10,2},{12,4},{14,6},{16,8},{18,10},{20,12},{22,14},{24,16},... | collective-permute-start | bytes 3194888 | tf_op jit(solution)/shard_map/ppermute | solution.py:22
  196.9 94.0 %collective-permute-start.9 = (bf16[520,1024]{1,0:T(8,128)(2,1)}, bf16[520,1024]{1,0:T(8,128)(2,1)}, u32[]{:S(2)}, u32[]{:S(2)}) collective-permute-start(bf16[520,1024]{1,0:T(8,128)(2,1)} %get-tuple-element.23), channel_id=1, source_target_pairs={{4,0},{6,2},{8,4},{10,6},{12,8},{14,10},{16,12},{18,14},{20,16},{2... | collective-permute-start | bytes 3194888 | tf_op jit(solution)/shard_map/ppermute | solution.py:22
  202.5 99.0 %copy-start.16 = (f32[260,384]{1,0:T(8,128)}, f32[260,384]{1,0:T(8,128)S(1)}, u32[]{:S(2)}) copy-start(f32[260,384]{1,0:T(8,128)S(1)} %reshape.107) | copy-start | bytes 1198084
  212.2 96.3 %collective-permute-start.8 = (bf16[260,1024]{1,0:T(8,128)(2,1)}, bf16[260,1024]{1,0:T(8,128)(2,1)}, u32[]{:S(2)}, u32[]{:S(2)}) collective-permute-start(bf16[260,1024]{1,0:T(8,128)(2,1)} %get-tuple-element.28), channel_id=1, source_target_pairs={{0,2},{2,4},{4,6},{6,8},{8,10},{10,12},{12,14},{14,16},{16,18},{18... | collective-permute-start | bytes 1597448 | tf_op jit(solution)/shard_map/ppermute | solution.py:22
  214.3 87.2 %copy-start.6 = (bf16[260,1536]{1,0:T(8,128)(2,1)S(1)}, bf16[260,1536]{1,0:T(8,128)(2,1)}, u32[]{:S(2)}) copy-start(bf16[260,1536]{1,0:T(8,128)(2,1)} %param.9) | copy-start | bytes 2396164
  214.3 87.2 %copy-start.15 = (f32[260,384]{1,0:T(8,128)S(1)}, f32[260,384]{1,0:T(8,128)}, u32[]{:S(2)}) copy-start(f32[260,384]{1,0:T(8,128)} %reshape.109) | copy-start | bytes 1198084
  214.3 87.2 %copy-start.17 = (f32[260,384]{1,0:T(8,128)S(1)}, f32[260,384]{1,0:T(8,128)}, u32[]{:S(2)}) copy-start(f32[260,384]{1,0:T(8,128)} %reshape.105) | copy-start | bytes 1198084
  214.4 87.2 %copy-start.18 = (f32[260,384]{1,0:T(8,128)S(1)}, f32[260,384]{1,0:T(8,128)}, u32[]{:S(2)}) copy-start(f32[260,384]{1,0:T(8,128)} %reshape.103) | copy-start | bytes 1198084
  214.4 94.1 %collective-permute-start.7 = (bf16[260,1024]{1,0:T(8,128)(2,1)}, bf16[260,1024]{1,0:T(8,128)(2,1)}, u32[]{:S(2)}, u32[]{:S(2)}) collective-permute-start(bf16[260,1024]{1,0:T(8,128)(2,1)} %get-tuple-element.27), channel_id=1, source_target_pairs={{2,0},{4,2},{6,4},{8,6},{10,8},{12,10},{14,12},{16,14},{18,16},{20... | collective-permute-start | bytes 1597448 | tf_op jit(solution)/shard_map/ppermute | solution.py:22
  296.0 16.8 %collective-permute-start.13 = (bf16[260,1024]{1,0:T(8,128)(2,1)}, bf16[260,1024]{1,0:T(8,128)(2,1)}, u32[]{:S(2)}, u32[]{:S(2)}) collective-permute-start(bf16[260,1024]{1,0:T(8,128)(2,1)} %get-tuple-element.30), channel_id=1, source_target_pairs={{0,2},{2,4},{4,6},{6,8},{8,10},{10,12},{12,14},{14,16},{16,18},{18... | collective-permute-start | bytes 1597448 | tf_op jit(solution)/shard_map/ppermute | solution.py:22
  297.9 14.9 %collective-permute-start.12 = (bf16[260,1024]{1,0:T(8,128)(2,1)}, bf16[260,1024]{1,0:T(8,128)(2,1)}, u32[]{:S(2)}, u32[]{:S(2)}) collective-permute-start(bf16[260,1024]{1,0:T(8,128)(2,1)} %get-tuple-element.29), channel_id=1, source_target_pairs={{2,0},{4,2},{6,4},{8,6},{10,8},{12,10},{14,12},{16,14},{18,16},{20... | collective-permute-start | bytes 1597448 | tf_op jit(solution)/shard_map/ppermute | solution.py:22
  309.9 11.5 %copy-start.36 = (f32[1536]{0:T(1024)S(1)}, f32[1536]{0:T(1024)}, u32[]{:S(2)}) copy-start(f32[1536]{0:T(1024)} %param.14) | copy-start | bytes 18436
  309.9 11.5 %copy-start.39 = (f32[260]{0:T(512)S(1)}, f32[260]{0:T(512)}, u32[]{:S(2)}) copy-start(f32[260]{0:T(512)} %copy-done.38) | copy-start | bytes 3124
  314.2 10.1 %copy-start.41 = (f32[260]{0:T(512)S(1)}, f32[260]{0:T(512)}, u32[]{:S(2)}) copy-start(f32[260]{0:T(512)} %copy-done.40) | copy-start | bytes 3124
  (37 other events, 129.4 us)
where the time goes:
time: 332 us; the launch traced here: 326 us
  waiting for transfers between devices  148 us (45%)
  matrix products  46.4 us (14%)
  other arithmetic  45.5 us (14%)
  starting transfers between devices  38 us (11%)
  local copies, waits for them, and re-layouts  32.7 us (10%)
  blocking collectives  10.6 us (3%)
  between operations  4.66 us (1%)
    ppermute x14, waiting for transfers between devices, shifted(): lax.ppermute(value, axis, [(source, source + steps) for source in range(i...  148 us
    ppermute x14, starting transfers between devices, shifted(): lax.ppermute(value, axis, [(source, source + steps) for source in range(i...  38 us
    dot_general x4, matrix products, attend(): jnp.dot(probs_low, value_columns, preferred_element_type=jnp.float32)  10.6 us
    dot_general x4, matrix products, attend(): jnp.dot(dscores, key_cols, preferred_element_type=jnp.float32)  9.91 us
    reduce_sum x1, other arithmetic, attend(): probs = weights / jnp.sum(weights, axis=1, keepdims=True)  8.69 us
    div x1, other arithmetic, attend(): probs = weights / jnp.sum(weights, axis=1, keepdims=True)  8.59 us
    dot_general x4, matrix products, attend(): lax.dot_general(out_grads, value_columns, (((1,), (1,)), ((), ())), prefe...  8.5 us
    dot_general x4, matrix products, attend(): lax.dot_general(query_rows, key_cols, (((1,), (1,)), ((), ())), preferred...  8.4 us
  transfers between devices with their start and end apart: 14, of which 10 were waited for; matrix products, arithmetic and copies ran while one was open for 13% of the time, Pallas kernels for 0%

commit v1 on v0

v1 whole, which is shorter than its diff:
```python
import functools
import math

import jax
import jax.numpy as jnp
from jax import lax
from jax.experimental import pallas as pl
from jax.experimental.pallas import tpu as pltpu
from jax.sharding import PartitionSpec as P

HEAD_SIZE = 128
KEY_VALUE_HEADS = 8
GROUP = 3
STRETCH = 520
WINDOW = 3
SLOTS = 2
HQ = 24

EPSILON = 1e-06
NEG_FILL = -1e30
LOG2E = 1.0 / math.log(2.0)
PIECES = 6


def padded_rows(rows):
    return -(-rows // 16) * 16


def permuted(value, pairs):
    return lax.ppermute(value, "seq", pairs)


def attend_kernel(raw_q, q_inv, gain, grad, bias, *refs):
    kv_refs = refs[:PIECES]
    out_ref, dq_ref = refs[PIECES : PIECES + 2]
    dkv_refs = refs[PIECES + 2 :]
    scale = HEAD_SIZE**-0.5
    keys = jnp.concatenate([ref[0] for ref in kv_refs], axis=0)
    values = jnp.concatenate([ref[1] for ref in kv_refs], axis=0)
    dk_total, dv_total = 0.0, 0.0
    for member in range(GROUP):
        cols = slice(member * HEAD_SIZE, (member + 1) * HEAD_SIZE)
        gain_row = gain[:, cols] * (scale * LOG2E)
        query = (raw_q[:, cols].astype(jnp.float32) * q_inv[...] * gain_row).astype(jnp.bfloat16)
        scores = lax.dot_general(
            query, keys, (((1,), (1,)), ((), ())), preferred_element_type=jnp.float32
        )
        scores = scores + bias[...]
        row_max = jnp.max(scores, axis=1, keepdims=True)
        weights = jnp.exp2(scores - row_max)
        inverse = 1.0 / jnp.sum(weights, axis=1, keepdims=True)
        weights_low = weights.astype(jnp.bfloat16)
        head_out = jnp.dot(weights_low, values, preferred_element_type=jnp.float32) * inverse
        out_ref[:, cols] = head_out.astype(out_ref.dtype)
        grad_rows = grad[:, cols].astype(jnp.float32) * inverse
        delta = jnp.sum(grad_rows * head_out, axis=1, keepdims=True)
        grad_low = grad_rows.astype(jnp.bfloat16)
        dprobs = lax.dot_general(
            grad_low, values, (((1,), (1,)), ((), ())), preferred_element_type=jnp.float32
        )
        dscores = (weights * (dprobs - delta)).astype(jnp.bfloat16)
        dq_ref[:, cols] = jnp.dot(dscores, keys, preferred_element_type=jnp.float32) * scale
        dk_total += lax.dot_general(
            dscores, query, (((0,), (0,)), ((), ())), preferred_element_type=jnp.float32
        )
        dv_total += lax.dot_general(
            weights_low, grad_low, (((0,), (0,)), ((), ())), preferred_element_type=jnp.float32
        )
    dk_total = dk_total * (1.0 / LOG2E)
    rows = kv_refs[0].shape[1]
    for index, ref in enumerate(dkv_refs):
        span = slice(index * rows, (index + 1) * rows)
        ref[0] = dk_total[span].astype(ref.dtype)
        ref[1] = dv_total[span].astype(ref.dtype)


def attend(noisy_q, q_inv, q_gain, out_grad, bias, pieces):
    rows, width = noisy_q.shape
    local_kv = width // (GROUP * HEAD_SIZE)
    piece_rows = pieces[0].shape[1]
    key_rows = PIECES * piece_rows
    group_cols = GROUP * HEAD_SIZE
    row_block = pl.BlockSpec((rows, group_cols), lambda j: (0, j))
    piece_block = pl.BlockSpec((2, piece_rows, HEAD_SIZE), lambda j: (0, 0, j))
    whole = lambda shape: pl.BlockSpec(shape, lambda j: (0, 0))
    flops = 2 * 6 * rows * GROUP * local_kv * key_rows * HEAD_SIZE
    return pl.pallas_call(
        attend_kernel,
        grid=(local_kv,),
        in_specs=[
            row_block,
            whole((rows, 1)),
            pl.BlockSpec((1, group_cols), lambda j: (0, j)),
            row_block,
            whole((1, key_rows)),
        ]
        + [piece_block] * PIECES,
        out_specs=[row_block, row_block] + [piece_block] * PIECES,
        out_shape=[
            jax.ShapeDtypeStruct((rows, width), jnp.bfloat16),
            jax.ShapeDtypeStruct((rows, width), jnp.float32),
        ]
        + [
            jax.ShapeDtypeStruct(pieces[0].shape, (jnp.float32, jnp.bfloat16)[i % 2])
            for i in range(PIECES)
        ],
        compiler_params=pltpu.CompilerParams(
            dimension_semantics=("arbitrary",), vmem_limit_bytes=56 * 1024 * 1024
        ),
        cost_estimate=pl.CostEstimate(
            flops=flops,
            bytes_accessed=16 * 1024 * 1024,
            transcendentals=rows * GROUP * local_kv * key_rows,
        ),
    )(noisy_q, q_inv, q_gain[None, :], out_grad, bias, *pieces)


def on_device(
    noisy_q, noisy_k, noisy_value, clean_k, clean_value, q_gain, key_norm_gain, out_grad, window
):
    rows = noisy_q.shape[0]
    count = lax.axis_size("seq")
    span = STRETCH // rows
    assert span == 2
    piece_rows = padded_rows(rows)
    pad = ((0, 0), (0, piece_rows - rows), (0, 0))
    stretch_id = lax.axis_index("seq") // span
    q_full = noisy_q.astype(jnp.float32)
    k_full = noisy_k.astype(jnp.float32)
    c_full = clean_k.astype(jnp.float32)
    totals = lax.psum(
        jnp.stack(
            [
                jnp.sum(q_full * q_full, axis=1),
                jnp.sum(k_full * k_full, axis=1),
                jnp.sum(c_full * c_full, axis=1),
            ]
        ),
        "head",
    )
    q_width = HQ * HEAD_SIZE
    key_width = KEY_VALUE_HEADS * HEAD_SIZE
    q_inv = lax.rsqrt(totals[0] / q_width + EPSILON)[:, None]
    k_inv = lax.rsqrt(totals[1] / key_width + EPSILON)[:, None]
    c_inv = lax.rsqrt(totals[2] / key_width + EPSILON)[:, None]
    k_norm = (k_full * k_inv * key_norm_gain[None, :]).astype(jnp.bfloat16)
    c_norm = (c_full * c_inv * key_norm_gain[None, :]).astype(jnp.bfloat16)
    noisy_own = jnp.pad(jnp.stack([k_norm, noisy_value]), pad)
    clean_own = jnp.pad(jnp.stack([c_norm, clean_value]), pad)

    partner = [(i, i ^ 1) for i in range(count)]
    ahead = lambda steps: [(i, i + steps * span) for i in range(count - steps * span)]
    back = lambda steps: [(i, i - steps * span) for i in range(steps * span, count)]

    ids = jnp.arange(window.shape[0], dtype=jnp.int32)
    low = jnp.min(window, axis=1)
    high = jnp.max(window, axis=1)
    pick = lambda table, at: jnp.sum(jnp.where(ids == at, table, 0))
    has_prev = pick(high, stretch_id) >= 0
    has_other = (pick(low, stretch_id) >= 0) & (pick(low, stretch_id) < pick(high, stretch_id))
    later_takes_own = pick(low, stretch_id + 2) == stretch_id

    prev_own = permuted(clean_own, ahead(1))
    noisy_par = permuted(noisy_own, partner)
    other_own = permuted(jnp.where(later_takes_own, clean_own, prev_own), ahead(2))
    prev_par = permuted(prev_own, partner)
    other_par = permuted(other_own, partner)

    real = jnp.arange(piece_rows) < rows
    flags = [True, True, has_prev, has_prev, has_other, has_other]
    bias = jnp.concatenate([jnp.where(real & flag, 0.0, NEG_FILL) for flag in flags])
    attn_out, dq_norm, dn_own, dn_par, dp_own, dp_par, do_own, do_par = attend(
        noisy_q,
        q_inv,
        q_gain,
        out_grad,
        bias[None, :].astype(jnp.float32),
        [noisy_own, noisy_par, prev_own, prev_par, other_own, other_par],
    )
    do_total = do_own + permuted(do_par, partner)
    dp_total = dp_own + permuted(dp_par, partner)
    dn_total = dn_own + permuted(dn_par, partner)
    from_later = permuted(do_total.astype(jnp.bfloat16), back(2)).astype(jnp.float32)
    dp_total = dp_total + jnp.where(later_takes_own, 0.0, from_later)
    from_next = permuted(dp_total.astype(jnp.bfloat16), back(1)).astype(jnp.float32)
    dc_total = from_next + jnp.where(later_takes_own, from_later, 0.0)

    q_scaled = dq_norm * q_gain[None, :]
    k_scaled = dn_total[0, :rows] * key_norm_gain[None, :]
    c_scaled = dc_total[0, :rows] * key_norm_gain[None, :]
    inner_sum = lax.psum(
        jnp.stack(
            [
                jnp.sum(q_scaled * q_full, axis=1),
                jnp.sum(k_scaled * k_full, axis=1),
                jnp.sum(c_scaled * c_full, axis=1),
            ]
        ),
        "head",
    )

    def norm_grad(full, inv, scaled, inner, width):
        return (inv * scaled - full * inv * inv * inv * (inner / width)[:, None]).astype(
            jnp.bfloat16
        )

    grad_q = norm_grad(q_full, q_inv, q_scaled, inner_sum[0], q_width)
    grad_k = norm_grad(k_full, k_inv, k_scaled, inner_sum[1], key_width)
    grad_clean_k = norm_grad(c_full, c_inv, c_scaled, inner_sum[2], key_width)
    grad_v = dn_total[1, :rows].astype(jnp.bfloat16)
    grad_clean_v = dc_total[1, :rows].astype(jnp.bfloat16)
    return (attn_out, grad_q, grad_k, grad_v, grad_clean_k, grad_clean_v)


def solution(mesh):
    split = P("seq", "head")
    return jax.shard_map(
        on_device,
        mesh=mesh,
        in_specs=(split, split, split, split, split, P("head"), P("head"), split, P()),
        out_specs=(split,) * 6,
        check_vma=False,
    )
```

time: 332 us -> 128 us (0.39)
  the two profiles are of different devices: /device:TPU:14 before, /device:TPU:0 now
where the time goes in v1:
time: 128 us
  waiting for transfers between devices  48.6 us (38%)
  Pallas kernels  30.3 us (24%)
  starting transfers between devices  13.9 us (11%)
  other arithmetic  13 us (10%)
  blocking collectives  11.6 us (9%)
  local copies, waits for them, and re-layouts  6.03 us (5%)
  between operations  4.33 us (3%)
    ppermute x10, waiting for transfers between devices, permuted(): return lax.ppermute(value, 'seq', pairs)  48.6 us
    pallas_call x1, Pallas kernels, attend(): pl.pallas_call(attend_kernel, grid=(local_kv,), in_specs=[row_block, whol...  30.3 us
    ppermute x10, starting transfers between devices, permuted(): return lax.ppermute(value, 'seq', pairs)  13.9 us
    psum x1, blocking collectives, on_device(): lax.psum(jnp.stack([jnp.sum(q_full * q_full, axis=1), jnp.sum(k_full * k_...  5.91 us
    psum x1, blocking collectives, on_device(): lax.psum(jnp.stack([jnp.sum(q_scaled * q_full, axis=1), jnp.sum(k_scaled...  5.68 us
    convert_element_type x2, other arithmetic, norm_grad(): (inv * scaled - full * inv * inv * inv * (inner / width)[:, None]).astype...  4.38 us
  transfers between devices with their start and end apart: 10, of which 5 were waited for; matrix products, arithmetic and copies ran while one was open for 5% of the time, Pallas kernels for 0%

profile of v1, /device:TPU:0, one launch (start us, length us, event | category | flops | bytes accessed | tf_op | source)
XLA Modules:
  0.0 127.7 jit_solution(15524745635506103710)
XLA Ops:
  0.7 1.5 %fusion = f32[260]{0:T(512)S(1)} fusion(bf16[260,1536]{1,0:T(8,128)(2,1)} %raw_q.1), kind=kLoop, calls=%fused_computation.3 | loop fusion | flops 1197820 | bytes 799760 | tf_op jit(solution)/shard_map/reduce_sum | solution.py:134
  2.1 1.1 fusion.30
  3.4 5.9 %psum.14 = f32[3,260]{1,0:T(4,128)S(1)} all-reduce(f32[3,260]{1,0:T(4,128)S(1)} %pad_maximum_fusion), channel_id=1, replica_groups=mesh['seq'=16,'head'=2] {'head'}, use_global_device_ids=true, to_apply=%region_3.4 | all-reduce | flops 780 | bytes 6240 | tf_op jit(solution)/shard_map/psum | solution.py:131
  9.3 0.6 fusion.59
  10.2 0.4 copy-done.19
  10.6 4.1 %collective-permute-start.1 = (bf16[2,272,512]{2,1,0:T(8,128)(2,1)S(1)}, bf16[2,272,512]{2,1,0:T(8,128)(2,1)S(1)}, u32[]{:S(2)}, u32[]{:S(2)}) collective-permute-start(bf16[2,272,512]{2,1,0:T(8,128)(2,1)S(1)} %fusion.19), channel_id=1, source_target_pairs={{0,4},{2,6},{4,8},{6,10},{8,12},{10,14},{12,16},{14,18},{16,20},{1... | collective-permute-start | bytes 1671176 | tf_op jit(solution)/shard_map/ppermute | solution.py:30
  14.8 0.7 fusion.58
  16.1 9.3 %collective-permute-done.1.refs_2_ = bf16[2,272,512]{2,1,0:T(8,128)(2,1)S(1)} collective-permute-done((bf16[2,272,512]{2,1,0:T(8,128)(2,1)S(1)}, bf16[2,272,512]{2,1,0:T(8,128)(2,1)S(1)}, u32[]{:S(2)}, u32[]{:S(2)}) %collective-permute-start.1) | collective-permute-done | bytes 557088 | tf_op jit(solution)/shard_map/ppermute | solution.py:30
  25.6 5.4 %collective-permute-start.3 = (bf16[2,272,512]{2,1,0:T(8,128)(2,1)S(1)}, bf16[2,272,512]{2,1,0:T(8,128)(2,1)S(1)}, u32[]{:S(2)}, u32[]{:S(2)}) collective-permute-start(bf16[2,272,512]{2,1,0:T(8,128)(2,1)S(1)} %broadcast_select_fusion), channel_id=1, source_target_pairs={{0,8},{2,10},{4,12},{6,14},{8,16},{10,18},{12,20},{14,22},{16,24},... | collective-permute-start | bytes 1671176 | tf_op jit(solution)/shard_map/ppermute | solution.py:30
  31.1 0.5 collective-permute-start.2
  31.6 9.1 %collective-permute-done.3.refs_4_ = bf16[2,272,512]{2,1,0:T(8,128)(2,1)S(1)} collective-permute-done((bf16[2,272,512]{2,1,0:T(8,128)(2,1)S(1)}, bf16[2,272,512]{2,1,0:T(8,128)(2,1)S(1)}, u32[]{:S(2)}, u32[]{:S(2)}) %collective-permute-start.3) | collective-permute-done | bytes 557088 | tf_op jit(solution)/shard_map/ppermute | solution.py:30
  43.5 0.6 broadcast_in_dim.53.bias
  44.1 0.6 broadcast_in_dim.49.gain
  44.7 0.8 copy.15.q_inv
  45.5 0.8 copy-done.25
  46.5 30.3 %shard_map.136 = (bf16[260,1536]{1,0:T(8,128)(2,1)}, f32[260,1536]{1,0:T(8,128)}, f32[2,272,512]{2,1,0:T(8,128)}, bf16[2,272,512]{2,1,0:T(8,128)(2,1)}, f32[2,27...) custom-call(bf16[260,1536]{1,0:T(8,128)(2,1)} %raw_q.1, ...), custom_call_target="tpu_custom_call" | custom-call | flops 7821066240 | bytes 16777216 | tf_op jit(solution)/shard_map/pallas_call | solution.py:87
  76.8 0.6 collective-permute-start.7
  77.4 1.7 %collective-permute-done.7 = bf16[2,272,512]{2,1,0:T(8,128)(2,1)S(1)} collective-permute-done((bf16[2,272,512]{2,1,0:T(8,128)(2,1)}, bf16[2,272,512]{2,1,0:T(8,128)(2,1)S(1)}, u32[]{:S(2)}, u32[]{:S(2)}) %collective-permute-start.7) | collective-permute-done | bytes 557088 | tf_op jit(solution)/shard_map/ppermute | solution.py:30
  79.2 1.5 %add_convert_fusion = bf16[2,272,512]{2,1,0:T(8,128)(2,1)S(1)} fusion(f32[2,272,512]{2,1,0:T(8,128)} %get-tuple-element.20, bf16[2,272,512]{2,1,0:T(8,128)(2,1)S(1)} %collective-permute-done.7), kind=kLoop, calls=%fused_computation.20 | loop fusion | flops 835584 | bytes 2228224 | tf_op jit(solution)/shard_map/convert_element_type | solution.py:183
  80.7 1.3 %collective-permute-start.8 = (bf16[2,272,512]{2,1,0:T(8,128)(2,1)S(1)}, bf16[2,272,512]{2,1,0:T(8,128)(2,1)S(1)}, u32[]{:S(2)}, u32[]{:S(2)}) collective-permute-start(bf16[2,272,512]{2,1,0:T(8,128)(2,1)S(1)} %add_convert_fusion), channel_id=1, source_target_pairs={{8,0},{10,2},{12,4},{14,6},{16,8},{18,10},{20,12},{22,14},{24,16},... | collective-permute-start | bytes 1671176 | tf_op jit(solution)/shard_map/ppermute | solution.py:30
  82.0 0.4 collective-permute-start.5
  82.5 15.8 %collective-permute-done.8 = bf16[2,272,512]{2,1,0:T(8,128)(2,1)S(1)} collective-permute-done((bf16[2,272,512]{2,1,0:T(8,128)(2,1)S(1)}, bf16[2,272,512]{2,1,0:T(8,128)(2,1)S(1)}, u32[]{:S(2)}, u32[]{:S(2)}) %collective-permute-start.8) | collective-permute-done | bytes 557088 | tf_op jit(solution)/shard_map/ppermute | solution.py:30
  98.5 1.4 %collective-permute-start.9 = (bf16[2,272,512]{2,1,0:T(8,128)(2,1)S(1)}, bf16[2,272,512]{2,1,0:T(8,128)(2,1)S(1)}, u32[]{:S(2)}, u32[]{:S(2)}) collective-permute-start(bf16[2,272,512]{2,1,0:T(8,128)(2,1)S(1)} %fusion.8), channel_id=1, source_target_pairs={{4,0},{6,2},{8,4},{10,6},{12,8},{14,10},{16,12},{18,14},{20,16},{2... | collective-permute-start | bytes 1671176 | tf_op jit(solution)/shard_map/ppermute | solution.py:30
  100.3 0.9 copy-done.9
  101.4 0.8 fusion.36
  102.2 12.6 %collective-permute-done.9 = bf16[2,272,512]{2,1,0:T(8,128)(2,1)S(1)} collective-permute-done((bf16[2,272,512]{2,1,0:T(8,128)(2,1)S(1)}, bf16[2,272,512]{2,1,0:T(8,128)(2,1)S(1)}, u32[]{:S(2)}, u32[]{:S(2)}) %collective-permute-start.9) | collective-permute-done | bytes 557088 | tf_op jit(solution)/shard_map/ppermute | solution.py:30
  115.3 0.7 fusion.37
  116.1 0.6 pad_maximum_fusion.1
  116.7 5.7 %psum.15 = f32[3,260]{1,0:T(4,128)} all-reduce(f32[3,260]{1,0:T(4,128)} %pad_maximum_fusion.1), channel_id=1, replica_groups=mesh['seq'=16,'head'=2] {'head'}, use_global_device_ids=true, to_apply=%region_12.13 | all-reduce | flops 780 | bytes 6240 | tf_op jit(solution)/shard_map/psum | solution.py:191
  122.4 0.8 fusion.45
  123.3 2.2 %fusion.5 = bf16[260,1536]{1,0:T(8,128)(2,1)} fusion(bf16[260,1536]{1,0:T(8,128)(2,1)S(1)} %copy-done, f32[260,1536]{1,0:T(8,128)S(1)} %copy-done.1, f32[260]{0:T(512)S(1)} %get-tuple-element.24, f32[1536]{0:T(1024)S(1)} %copy-done.15, f32[260]{0:T(512)} %get-tuple-element.25), kind=kLoop, calls=%fused_computation.8 | loop fusion | flops 3594240 | bytes 3203104 | tf_op jit(solution)/shard_map/convert_element_type | solution.py:203
  125.5 2.2 %fusion.24 = (bf16[260,512]{1,0:T(8,128)(2,1)}, bf16[260,512]{1,0:T(8,128)(2,1)}) fusion(bf16[260,512]{1,0:T(8,128)(2,1)S(1)} %copy-done.5, f32[2,272,512]{2,1,0:T(8,128)S(1)} %fusion.9, f32[260]{0:T(512)S(1)} %get-tuple-element.22, f32[260]{0:T(512)S(1)} %copy-done.20, f32[512]{0:T(512)S(1)} %copy-done.18, f32[260]{0:T(512)S(1)} %get-tuple-element.23, ...), kind=kLoop, calls=%fused_computation.39 | loop fusion | flops 2396160 | bytes 2136128 | tf_op jit(solution)/shard_map/convert_element_type | solution.py:203
  (83 shorter events, 2.4 us)
Async XLA Ops:
  0.6 9.3 %copy-start.6 = (bf16[260,512]{1,0:T(8,128)(2,1)S(1)}, bf16[260,512]{1,0:T(8,128)(2,1)}, u32[]{:S(2)}) copy-start(bf16[260,512]{1,0:T(8,128)(2,1)} %param.10) | copy-start | bytes 798724
  0.6 2.6 %copy-start.3 = (bf16[260,512]{1,0:T(8,128)(2,1)S(1)}, bf16[260,512]{1,0:T(8,128)(2,1)}, u32[]{:S(2)}) copy-start(bf16[260,512]{1,0:T(8,128)(2,1)} %param.12) | copy-start | bytes 798724
  0.7 9.3 %copy-start.16 = (f32[512]{0:T(512)S(1)}, f32[512]{0:T(512)}, u32[]{:S(2)}) copy-start(f32[512]{0:T(512)} %param.15) | copy-start | bytes 6148
  0.7 9.9 %copy-start.11 = (bf16[260,512]{1,0:T(8,128)(2,1)S(1)}, bf16[260,512]{1,0:T(8,128)(2,1)}, u32[]{:S(2)}) copy-start(bf16[260,512]{1,0:T(8,128)(2,1)} %param.13) | copy-start | bytes 798724
  10.0 4.8 %copy-start.21 = (f32[260]{0:T(512)}, f32[260]{0:T(512)S(1)}, u32[]{:S(2)}) copy-start(f32[260]{0:T(512)S(1)} %get-tuple-element.27) | copy-start | bytes 3124
  10.0 4.8 %copy-start.23 = (s32[8,2]{0,1:T(2,128)S(1)}, s32[8,2]{0,1:T(2,128)}, u32[]{:S(2)}) copy-start(s32[8,2]{0,1:T(2,128)} %param.17) | copy-start | bytes 196
  10.6 20.4 %copy-start.14 = (bf16[260,512]{1,0:T(8,128)(2,1)S(1)}, bf16[260,512]{1,0:T(8,128)(2,1)}, u32[]{:S(2)}) copy-start(bf16[260,512]{1,0:T(8,128)(2,1)} %param.11) | copy-start | bytes 798724
  10.6 14.8 %collective-permute-start.1 = (bf16[2,272,512]{2,1,0:T(8,128)(2,1)S(1)}, bf16[2,272,512]{2,1,0:T(8,128)(2,1)S(1)}, u32[]{:S(2)}, u32[]{:S(2)}) collective-permute-start(bf16[2,272,512]{2,1,0:T(8,128)(2,1)S(1)} %fusion.19), channel_id=1, source_target_pairs={{0,4},{2,6},{4,8},{6,10},{8,12},{10,14},{12,16},{14,18},{16,20},{1... | collective-permute-start | bytes 1671176 | tf_op jit(solution)/shard_map/ppermute | solution.py:30
  16.1 27.9 %copy-start.15 = (f32[1536]{0:T(1024)S(1)}, f32[1536]{0:T(1024)}, u32[]{:S(2)}) copy-start(f32[1536]{0:T(1024)} %param.14) | copy-start | bytes 18436
  25.4 5.7 %copy-start.12 = (bf16[2,272,512]{2,1,0:T(8,128)(2,1)}, bf16[2,272,512]{2,1,0:T(8,128)(2,1)S(1)}, u32[]{:S(2)}) copy-start(bf16[2,272,512]{2,1,0:T(8,128)(2,1)S(1)} %collective-permute-done.1.refs_2_) | copy-start | bytes 1671172
  25.6 15.1 %collective-permute-start.3 = (bf16[2,272,512]{2,1,0:T(8,128)(2,1)S(1)}, bf16[2,272,512]{2,1,0:T(8,128)(2,1)S(1)}, u32[]{:S(2)}, u32[]{:S(2)}) collective-permute-start(bf16[2,272,512]{2,1,0:T(8,128)(2,1)S(1)} %broadcast_select_fusion), channel_id=1, source_target_pairs={{0,8},{2,10},{4,12},{6,14},{8,16},{10,18},{12,20},{14,22},{16,24},... | collective-permute-start | bytes 1671176 | tf_op jit(solution)/shard_map/ppermute | solution.py:30
  31.0 14.5 %copy-start.13 = (bf16[2,272,512]{2,1,0:T(8,128)(2,1)}, bf16[2,272,512]{2,1,0:T(8,128)(2,1)S(1)}, u32[]{:S(2)}) copy-start(bf16[2,272,512]{2,1,0:T(8,128)(2,1)S(1)} %fusion.18.refs_0_) | copy-start | bytes 1671172
  31.0 14.4 %collective-permute-start = (bf16[2,272,512]{2,1,0:T(8,128)(2,1)S(1)}, bf16[2,272,512]{2,1,0:T(8,128)(2,1)S(1)}, u32[]{:S(2)}, u32[]{:S(2)}) collective-permute-start(bf16[2,272,512]{2,1,0:T(8,128)(2,1)S(1)} %fusion.18.refs_0_), channel_id=1, source_target_pairs={{0,2},{2,0},{4,6},{6,4},{8,10},{10,8},{12,14},{14,12},{16,18},{18,... | collective-permute-start | bytes 1671176 | tf_op jit(solution)/shard_map/ppermute | solution.py:30
  31.1 14.3 %collective-permute-start.2 = (bf16[2,272,512]{2,1,0:T(8,128)(2,1)S(1)}, bf16[2,272,512]{2,1,0:T(8,128)(2,1)S(1)}, u32[]{:S(2)}, u32[]{:S(2)}) collective-permute-start(bf16[2,272,512]{2,1,0:T(8,128)(2,1)S(1)} %collective-permute-done.1.refs_2_), channel_id=1, source_target_pairs={{0,2},{2,0},{4,6},{6,4},{8,10},{10,8},{12,14},{14,12},{16,18},{18,... | collective-permute-start | bytes 1671176 | tf_op jit(solution)/shard_map/ppermute | solution.py:30
  40.7 4.8 %copy-start.24 = (bf16[2,272,512]{2,1,0:T(8,128)(2,1)}, bf16[2,272,512]{2,1,0:T(8,128)(2,1)S(1)}, u32[]{:S(2)}) copy-start(bf16[2,272,512]{2,1,0:T(8,128)(2,1)S(1)} %collective-permute-done.3.refs_4_) | copy-start | bytes 1671172
  40.7 4.8 %collective-permute-start.4 = (bf16[2,272,512]{2,1,0:T(8,128)(2,1)S(1)}, bf16[2,272,512]{2,1,0:T(8,128)(2,1)}, u32[]{:S(2)}, u32[]{:S(2)}) collective-permute-start(bf16[2,272,512]{2,1,0:T(8,128)(2,1)S(1)} %collective-permute-done.3.refs_4_), channel_id=1, source_target_pairs={{0,2},{2,0},{4,6},{6,4},{8,10},{10,8},{12,14},{14,12},{16,18},{18,... | collective-permute-start | bytes 1671176 | tf_op jit(solution)/shard_map/ppermute | solution.py:30
  76.8 2.4 %collective-permute-start.7 = (bf16[2,272,512]{2,1,0:T(8,128)(2,1)}, bf16[2,272,512]{2,1,0:T(8,128)(2,1)S(1)}, u32[]{:S(2)}, u32[]{:S(2)}) collective-permute-start(bf16[2,272,512]{2,1,0:T(8,128)(2,1)} %get-tuple-element.21), channel_id=1, source_target_pairs={{0,2},{2,0},{4,6},{6,4},{8,10},{10,8},{12,14},{14,12},{16,18},{18,... | collective-permute-start | bytes 1671176 | tf_op jit(solution)/shard_map/ppermute | solution.py:30
  77.4 5.1 %collective-permute-start.6 = (bf16[2,272,512]{2,1,0:T(8,128)(2,1)}, bf16[2,272,512]{2,1,0:T(8,128)(2,1)S(1)}, u32[]{:S(2)}, u32[]{:S(2)}) collective-permute-start(bf16[2,272,512]{2,1,0:T(8,128)(2,1)} %get-tuple-element.19), channel_id=1, source_target_pairs={{0,2},{2,0},{4,6},{6,4},{8,10},{10,8},{12,14},{14,12},{16,18},{18,... | collective-permute-start | bytes 1671176 | tf_op jit(solution)/shard_map/ppermute | solution.py:30
  79.2 2.9 %copy-start.27 = (bf16[2,272,512]{2,1,0:T(8,128)(2,1)S(1)}, bf16[2,272,512]{2,1,0:T(8,128)(2,1)}, u32[]{:S(2)}) copy-start(bf16[2,272,512]{2,1,0:T(8,128)(2,1)} %get-tuple-element.17) | copy-start | bytes 1671172
  79.2 19.1 %copy-start.10 = (f32[2,272,512]{2,1,0:T(8,128)S(1)}, f32[2,272,512]{2,1,0:T(8,128)}, u32[]{:S(2)}) copy-start(f32[2,272,512]{2,1,0:T(8,128)} %get-tuple-element.18) | copy-start | bytes 3342340
  80.7 17.5 %collective-permute-start.8 = (bf16[2,272,512]{2,1,0:T(8,128)(2,1)S(1)}, bf16[2,272,512]{2,1,0:T(8,128)(2,1)S(1)}, u32[]{:S(2)}, u32[]{:S(2)}) collective-permute-start(bf16[2,272,512]{2,1,0:T(8,128)(2,1)S(1)} %add_convert_fusion), channel_id=1, source_target_pairs={{8,0},{10,2},{12,4},{14,6},{16,8},{18,10},{20,12},{22,14},{24,16},... | collective-permute-start | bytes 1671176 | tf_op jit(solution)/shard_map/ppermute | solution.py:30
  82.0 18.3 %collective-permute-start.5 = (bf16[2,272,512]{2,1,0:T(8,128)(2,1)S(1)}, bf16[2,272,512]{2,1,0:T(8,128)(2,1)S(1)}, u32[]{:S(2)}, u32[]{:S(2)}) collective-permute-start(bf16[2,272,512]{2,1,0:T(8,128)(2,1)S(1)} %copy-done.27), channel_id=1, source_target_pairs={{0,2},{2,0},{4,6},{6,4},{8,10},{10,8},{12,14},{14,12},{16,18},{18,... | collective-permute-start | bytes 1671176 | tf_op jit(solution)/shard_map/ppermute | solution.py:30
  98.5 16.4 %collective-permute-start.9 = (bf16[2,272,512]{2,1,0:T(8,128)(2,1)S(1)}, bf16[2,272,512]{2,1,0:T(8,128)(2,1)S(1)}, u32[]{:S(2)}, u32[]{:S(2)}) collective-permute-start(bf16[2,272,512]{2,1,0:T(8,128)(2,1)S(1)} %fusion.8), channel_id=1, source_target_pairs={{4,0},{6,2},{8,4},{10,6},{12,8},{14,10},{16,12},{18,14},{20,16},{2... | collective-permute-start | bytes 1671176 | tf_op jit(solution)/shard_map/ppermute | solution.py:30
  101.4 13.7 %copy-start.2 = (f32[2,272,512]{2,1,0:T(8,128)}, f32[2,272,512]{2,1,0:T(8,128)S(1)}, u32[]{:S(2)}) copy-start(f32[2,272,512]{2,1,0:T(8,128)S(1)} %convert_add_fusion) | copy-start | bytes 3342340
  102.2 12.8 %copy-start.4 = (bf16[260,512]{1,0:T(8,128)(2,1)S(1)}, bf16[260,512]{1,0:T(8,128)(2,1)}, u32[]{:S(2)}) copy-start(bf16[260,512]{1,0:T(8,128)(2,1)} %param.12) | copy-start | bytes 798724
  102.2 12.9 %copy-start.7 = (bf16[260,512]{1,0:T(8,128)(2,1)S(1)}, bf16[260,512]{1,0:T(8,128)(2,1)}, u32[]{:S(2)}) copy-start(bf16[260,512]{1,0:T(8,128)(2,1)} %param.10) | copy-start | bytes 798724
  102.2 12.9 %copy-start.17 = (f32[512]{0:T(512)S(1)}, f32[512]{0:T(512)}, u32[]{:S(2)}) copy-start(f32[512]{0:T(512)} %param.15) | copy-start | bytes 6148
  123.2 2.2 %copy-start.5 = (bf16[260,512]{1,0:T(8,128)(2,1)S(1)}, bf16[260,512]{1,0:T(8,128)(2,1)}, u32[]{:S(2)}) copy-start(bf16[260,512]{1,0:T(8,128)(2,1)} %param.12) | copy-start | bytes 798724
  123.2 2.2 %copy-start.8 = (bf16[260,512]{1,0:T(8,128)(2,1)S(1)}, bf16[260,512]{1,0:T(8,128)(2,1)}, u32[]{:S(2)}) copy-start(bf16[260,512]{1,0:T(8,128)(2,1)} %param.10) | copy-start | bytes 798724
  123.2 2.2 %copy-start.18 = (f32[512]{0:T(512)S(1)}, f32[512]{0:T(512)}, u32[]{:S(2)}) copy-start(f32[512]{0:T(512)} %param.15) | copy-start | bytes 6148
  123.2 2.2 %copy-start.20 = (f32[260]{0:T(512)S(1)}, f32[260]{0:T(512)}, u32[]{:S(2)}) copy-start(f32[260]{0:T(512)} %copy-done.19) | copy-start | bytes 3124
  123.2 2.2 %copy-start.22 = (f32[260]{0:T(512)S(1)}, f32[260]{0:T(512)}, u32[]{:S(2)}) copy-start(f32[260]{0:T(512)} %copy-done.21) | copy-start | bytes 3124
  (6 other events, 7.0 us)

commit v2 on v1

v2 whole, which is shorter than its diff:
```python
import math

import jax
import jax.numpy as jnp
from jax import lax
from jax.experimental import pallas as pl
from jax.experimental.pallas import tpu as pltpu
from jax.sharding import PartitionSpec as P

HEAD_SIZE = 128
KEY_VALUE_HEADS = 8
GROUP = 3
STRETCH = 520
WINDOW = 3
SLOTS = 2
HQ = 24

EPSILON = 1e-06
NEG_FILL = -1e30
LOG2E = 1.0 / math.log(2.0)
PIECES = 6


def padded_rows(rows):
    return -(-rows // 16) * 16


def key_pieces(bufs, head, part):
    return jnp.concatenate([buf[head, part] for buf in bufs], axis=0)


def stretch_kernel(
    raw_q,
    q_inv,
    q_gain,
    grad,
    bias,
    raw_k,
    value,
    k_inv,
    raw_c,
    clean_value,
    c_inv,
    key_gain,
    take_own,
    out_ref,
    dq_ref,
    dk_ref,
    dv_ref,
    dck_ref,
    dcv_ref,
    noisy_own,
    clean_own,
    noisy_par,
    prev_own,
    prev_par,
    relay,
    other_own,
    other_par,
    grad_own,
    grad_out,
    grad_in,
    later_out,
    later_in,
    next_out,
    next_in,
    send_sems,
    recv_sems,
):
    heads = noisy_own.shape[0]
    rows = raw_q.shape[0]
    piece_rows = noisy_own.shape[2]
    scale = HEAD_SIZE**-0.5
    here = lax.axis_index("seq")
    count = lax.axis_size("seq")
    partner = here + 1 - 2 * (here % 2)
    ahead = lambda steps: (here + 2 * steps) % count
    back = lambda steps: (here + count - 2 * steps) % count

    barrier = pltpu.get_barrier_semaphore()
    peers = (partner, ahead(1), ahead(2), back(1), back(2))
    for peer in peers:
        pl.semaphore_signal(
            barrier, inc=1, device_id={"seq": peer}, device_id_type=pl.DeviceIdType.MESH
        )

    def copy(kind, head, src, dst, target):
        return pltpu.make_async_remote_copy(
            src_ref=src.at[head],
            dst_ref=dst.at[head],
            send_sem=send_sems.at[kind, head],
            recv_sem=recv_sems.at[kind, head],
            device_id={"seq": target},
            device_id_type=pl.DeviceIdType.MESH,
        )

    clean_next = lambda h: copy(0, h, clean_own, prev_own, ahead(1))
    noisy_pair = lambda h: copy(1, h, noisy_own, noisy_par, partner)
    prev_pair = lambda h: copy(2, h, prev_own, prev_par, partner)
    clean_later = lambda h: copy(3, h, relay, other_own, ahead(2))
    other_pair = lambda h: copy(4, h, other_own, other_par, partner)
    grad_pair = lambda h: copy(5, h, grad_out, grad_in, partner)
    grad_later = lambda h: copy(6, h, later_out, later_in, back(2))
    grad_next = lambda h: copy(7, h, next_out, next_in, back(1))
    kinds = (
        clean_next,
        noisy_pair,
        prev_pair,
        clean_later,
        other_pair,
        grad_pair,
        grad_later,
        grad_next,
    )

    noisy_own[...] = jnp.zeros_like(noisy_own)
    clean_own[...] = jnp.zeros_like(clean_own)
    for h in range(heads):
        cols = slice(h * HEAD_SIZE, (h + 1) * HEAD_SIZE)
        gain_row = key_gain[:, cols]
        clean_own[h, 0, :rows] = (raw_c[:, cols].astype(jnp.float32) * c_inv[...] * gain_row).astype(
            jnp.bfloat16
        )
        clean_own[h, 1, :rows] = clean_value[:, cols]
        if h == 0:
            pl.semaphore_wait(barrier, len(peers))
        if h < 2:
            clean_next(h).start()
        noisy_own[h, 0, :rows] = (raw_k[:, cols].astype(jnp.float32) * k_inv[...] * gain_row).astype(
            jnp.bfloat16
        )
        noisy_own[h, 1, :rows] = value[:, cols]
        noisy_pair(h).start()

    def pass_clean(h):
        clean_next(h).wait_recv()
        prev_pair(h).start()
        own = clean_own[h].astype(jnp.float32)
        prev = prev_own[h].astype(jnp.float32)
        relay[h] = jnp.where(take_own[...] > 0.0, own, prev).astype(jnp.bfloat16)
        clean_later(h).start()

    def pass_other(h):
        clean_later(h).wait_recv()
        other_pair(h).start()

    def pass_grads(h):
        grad_pair(h).wait_recv()
        later_out[h] = (grad_own[h, 2] + grad_in[h, 2].astype(jnp.float32)).astype(jnp.bfloat16)
        grad_later(h).start()
        cols = pl.ds(pl.multiple_of(h * HEAD_SIZE, HEAD_SIZE), HEAD_SIZE)
        total = grad_own[h, 0] + grad_in[h, 0].astype(jnp.float32)
        dk_ref[:, cols] = total[0]
        dv_ref[:, cols] = total[1].astype(jnp.bfloat16)
        grad_own[h, 1] = grad_own[h, 1] + grad_in[h, 1].astype(jnp.float32)

    def pass_later(h):
        grad_later(h).wait_recv()
        arrived = later_in[h].astype(jnp.float32)
        own = take_own[...] > 0.0
        next_out[h] = (grad_own[h, 1] + jnp.where(own, 0.0, arrived)).astype(jnp.bfloat16)
        grad_next(h).start()

    def finish(h):
        grad_next(h).wait_recv()
        own = take_own[...] > 0.0
        total = next_in[h].astype(jnp.float32) + jnp.where(
            own, later_in[h].astype(jnp.float32), 0.0
        )
        cols = pl.ds(pl.multiple_of(h * HEAD_SIZE, HEAD_SIZE), HEAD_SIZE)
        dck_ref[:, cols] = total[0]
        dcv_ref[:, cols] = total[1].astype(jnp.bfloat16)

    for h in range(min(2, heads)):
        pass_clean(h)
        if h + 2 < heads:
            clean_next(h + 2).start()
    pass_other(0)

    own_par = (noisy_own, noisy_par, prev_own, prev_par, other_own, other_par)

    def step(h, carry):
        noisy_pair(h).wait_recv()
        prev_pair(h).wait_recv()
        other_pair(h).wait_recv()
        keys = key_pieces(own_par, h, 0)
        values = key_pieces(own_par, h, 1)
        dk_total, dv_total = 0.0, 0.0
        for member in range(GROUP):
            first = pl.multiple_of((h * GROUP + member) * HEAD_SIZE, HEAD_SIZE)
            cols = pl.ds(first, HEAD_SIZE)
            gain_row = q_gain[:, cols] * (scale * LOG2E)
            query = (raw_q[:, cols].astype(jnp.float32) * q_inv[...] * gain_row).astype(
                jnp.bfloat16
            )
            scores = lax.dot_general(
                query, keys, (((1,), (1,)), ((), ())), preferred_element_type=jnp.float32
            )
            scores = scores + bias[...]
            row_max = jnp.max(scores, axis=1, keepdims=True)
            weights = jnp.exp2(scores - row_max)
            inverse = 1.0 / jnp.sum(weights, axis=1, keepdims=True)
            weights_low = weights.astype(jnp.bfloat16)
            head_out = jnp.dot(weights_low, values, preferred_element_type=jnp.float32) * inverse
            out_ref[:, cols] = head_out.astype(out_ref.dtype)
            grad_rows = grad[:, cols].astype(jnp.float32) * inverse
            delta = jnp.sum(grad_rows * head_out, axis=1, keepdims=True)
            grad_low = grad_rows.astype(jnp.bfloat16)
            dprobs = lax.dot_general(
                grad_low, values, (((1,), (1,)), ((), ())), preferred_element_type=jnp.float32
            )
            dscores = (weights * (dprobs - delta)).astype(jnp.bfloat16)
            dq_ref[:, cols] = jnp.dot(dscores, keys, preferred_element_type=jnp.float32) * scale
            dk_total += lax.dot_general(
                dscores, query, (((0,), (0,)), ((), ())), preferred_element_type=jnp.float32
            )
            dv_total += lax.dot_general(
                weights_low, grad_low, (((0,), (0,)), ((), ())), preferred_element_type=jnp.float32
            )
            if member == 0:
                pl.when(h + 2 < heads)(lambda: pass_clean(h + 2))
                pl.when(h >= 1)(lambda: pass_grads(h - 1))
            if member == 1:
                pl.when(h + 1 < heads)(lambda: pass_other(h + 1))
                pl.when(h >= 2)(lambda: pass_later(h - 2))
        dk_total = dk_total * (1.0 / LOG2E)
        for index in range(PIECES // 2):
            for part, total in enumerate((dk_total, dv_total)):
                at = 2 * index * piece_rows
                grad_own[h, index, part] = total[at : at + piece_rows]
                grad_out[h, index, part] = total[at + piece_rows : at + 2 * piece_rows].astype(
                    jnp.bfloat16
                )
        grad_pair(h).start()
        return carry

    lax.fori_loop(0, heads, step, 0)
    pass_grads(heads - 1)
    for h in range(max(heads - 2, 0), heads):
        pass_later(h)
    for h in range(heads):
        finish(h)
    for kind in kinds:
        for h in range(heads):
            kind(h).wait_send()


def attend(raw_q, q_inv, q_gain, grad, bias, raw_k, value, k_inv, raw_c, clean_value, c_inv, key_gain, take_own):
    rows, width = raw_q.shape
    heads = raw_k.shape[1] // HEAD_SIZE
    piece_rows = padded_rows(rows)
    key_rows = PIECES * piece_rows
    piece = pltpu.VMEM((heads, 2, piece_rows, HEAD_SIZE), jnp.bfloat16)
    triple = (heads, 3, 2, piece_rows, HEAD_SIZE)
    key_out = (piece_rows, heads * HEAD_SIZE)
    args = (
        raw_q,
        q_inv,
        q_gain[None, :],
        grad,
        bias,
        raw_k,
        value,
        k_inv,
        raw_c,
        clean_value,
        c_inv,
        key_gain[None, :],
        take_own,
    )
    vmem = pl.BlockSpec(memory_space=pltpu.VMEM)
    return pl.pallas_call(
        stretch_kernel,
        in_specs=[vmem] * len(args),
        out_specs=[vmem] * 6,
        out_shape=[
            jax.ShapeDtypeStruct((rows, width), jnp.bfloat16),
            jax.ShapeDtypeStruct((rows, width), jnp.float32),
            jax.ShapeDtypeStruct(key_out, jnp.float32),
            jax.ShapeDtypeStruct(key_out, jnp.bfloat16),
            jax.ShapeDtypeStruct(key_out, jnp.float32),
            jax.ShapeDtypeStruct(key_out, jnp.bfloat16),
        ],
        scratch_shapes=[piece] * 8
        + [
            pltpu.VMEM(triple, jnp.float32),
            pltpu.VMEM(triple, jnp.bfloat16),
            pltpu.VMEM(triple, jnp.bfloat16),
        ]
        + [piece] * 4
        + [pltpu.SemaphoreType.DMA((8, heads)), pltpu.SemaphoreType.DMA((8, heads))],
        compiler_params=pltpu.CompilerParams(
            collective_id=0, has_side_effects=True, vmem_limit_bytes=58 * 1024 * 1024
        ),
        cost_estimate=pl.CostEstimate(
            flops=2 * 6 * rows * GROUP * heads * key_rows * HEAD_SIZE,
            bytes_accessed=16 * 1024 * 1024,
            transcendentals=rows * GROUP * heads * key_rows,
        ),
    )(*args)


def on_device(
    noisy_q, noisy_k, noisy_value, clean_k, clean_value, q_gain, key_norm_gain, out_grad, window
):
    rows = noisy_q.shape[0]
    span = STRETCH // rows
    assert span == 2
    piece_rows = padded_rows(rows)
    stretch_id = lax.axis_index("seq") // span
    q_full = noisy_q.astype(jnp.float32)
    k_full = noisy_k.astype(jnp.float32)
    c_full = clean_k.astype(jnp.float32)
    totals = lax.psum(
        jnp.stack(
            [
                jnp.sum(q_full * q_full, axis=1),
                jnp.sum(k_full * k_full, axis=1),
                jnp.sum(c_full * c_full, axis=1),
            ]
        ),
        "head",
    )
    q_width = HQ * HEAD_SIZE
    key_width = KEY_VALUE_HEADS * HEAD_SIZE
    q_inv = lax.rsqrt(totals[0] / q_width + EPSILON)[:, None]
    k_inv = lax.rsqrt(totals[1] / key_width + EPSILON)[:, None]
    c_inv = lax.rsqrt(totals[2] / key_width + EPSILON)[:, None]

    ids = jnp.arange(window.shape[0], dtype=jnp.int32)
    low = jnp.min(window, axis=1)
    high = jnp.max(window, axis=1)
    pick = lambda table, at: jnp.sum(jnp.where(ids == at, table, 0))
    has_prev = pick(high, stretch_id) >= 0
    has_other = (pick(low, stretch_id) >= 0) & (pick(low, stretch_id) < pick(high, stretch_id))
    later_takes_own = pick(low, stretch_id + 2) == stretch_id

    real = jnp.arange(piece_rows) < rows
    flags = [True, True, has_prev, has_prev, has_other, has_other]
    bias = jnp.concatenate([jnp.where(real & flag, 0.0, NEG_FILL) for flag in flags])
    attn_out, dq_norm, dk_norm, grad_v, dc_norm, grad_clean_v = attend(
        noisy_q,
        q_inv,
        q_gain,
        out_grad,
        bias[None, :].astype(jnp.float32),
        noisy_k,
        noisy_value,
        k_inv,
        clean_k,
        clean_value,
        c_inv,
        key_norm_gain,
        jnp.full((1, HEAD_SIZE), later_takes_own.astype(jnp.float32)),
    )

    q_scaled = dq_norm * q_gain[None, :]
    k_scaled = dk_norm[:rows] * key_norm_gain[None, :]
    c_scaled = dc_norm[:rows] * key_norm_gain[None, :]
    inner_sum = lax.psum(
        jnp.stack(
            [
                jnp.sum(q_scaled * q_full, axis=1),
                jnp.sum(k_scaled * k_full, axis=1),
                jnp.sum(c_scaled * c_full, axis=1),
            ]
        ),
        "head",
    )

    def norm_grad(full, inv, scaled, inner, width):
        return (inv * scaled - full * inv * inv * inv * (inner / width)[:, None]).astype(
            jnp.bfloat16
        )

    grad_q = norm_grad(q_full, q_inv, q_scaled, inner_sum[0], q_width)
    grad_k = norm_grad(k_full, k_inv, k_scaled, inner_sum[1], key_width)
    grad_clean_k = norm_grad(c_full, c_inv, c_scaled, inner_sum[2], key_width)
    return (attn_out, grad_q, grad_k, grad_v[:rows], grad_clean_k, grad_clean_v[:rows])


def solution(mesh):
    split = P("seq", "head")
    return jax.shard_map(
        on_device,
        mesh=mesh,
        in_specs=(split, split, split, split, split, P("head"), P("head"), split, P()),
        out_specs=(split,) * 6,
        check_vma=False,
    )
```

time: 128 us -> 100 us (0.78)
  waiting for transfers between devices: 48.6 us -> 0 us
  Pallas kernels: 30.3 us -> 64.2 us
  starting transfers between devices: 13.9 us -> 0 us
    ppermute x10 -> x0, waiting for transfers between devices: 48.6 us -> none  [permuted(): return lax.ppermute(value, 'seq', pairs)]
    pallas_call x1, Pallas kernels: 30.3 us -> 64.2 us  [attend(): pl.pallas_call(stretch_kernel, in_specs=[vmem] * len(args), out_specs=[vm...]
    ppermute x10 -> x0, starting transfers between devices: 13.9 us -> none  [permuted(): return lax.ppermute(value, 'seq', pairs)]
    convert_element_type x2 -> x0, other arithmetic: 1.8 us -> none  [the longest x1 1.54 us: on_device(): do_total.astype(jnp.bfloat16)]
    rsqrt x0 -> x2, local copies, waits for them, and re-layouts: none -> 1.61 us  [the longest x1 0.8 us: on_device(): k_inv = lax.rsqrt(totals[1] / key_width + EPSILON)[:, None]]
    convert_element_type x2 -> x0, local copies, waits for them, and re-layouts: 1.55 us -> none  [the longest x1 0.81 us: on_device(): grad_v = dn_total[1, :rows].astype(jnp.bfloat16)]
    reduce_sum x1, other arithmetic: 0.3 us -> 1.8 us  [on_device(): jnp.sum(q_scaled * q_full, axis=1)]
    slice x0 -> x2, local copies, waits for them, and re-layouts: none -> 1.45 us  [the longest x1 0.72 us: on_device(): grad_v[:rows]]
  transfers between devices with their start and end apart: 10 -> 0, of which waited for: 5 -> 0; matrix products, arithmetic and copies ran while one was open for 5% -> 0% of each run, Pallas kernels for 0% -> 0%
where the time goes in v2:
time: 100 us; the launch traced here: 99.4 us
  Pallas kernels  64.2 us (64%)
  other arithmetic  13.4 us (13%)
  blocking collectives  11 us (11%)
  local copies, waits for them, and re-layouts  6.69 us (7%)
  between operations  4.05 us (4%)
    pallas_call x1, Pallas kernels, attend(): pl.pallas_call(stretch_kernel, in_specs=[vmem] * len(args), out_specs=[vm...  64.2 us
    psum x1, blocking collectives, on_device(): lax.psum(jnp.stack([jnp.sum(q_full * q_full, axis=1), jnp.sum(k_full * k_...  5.91 us
    psum x1, blocking collectives, on_device(): lax.psum(jnp.stack([jnp.sum(q_scaled * q_full, axis=1), jnp.sum(k_scaled...  5.13 us
    convert_element_type x2, other arithmetic, norm_grad(): (inv * scaled - full * inv * inv * inv * (inner / width)[:, None]).astype...  4.43 us

profile of v2, /device:TPU:0, one launch (start us, length us, event | category | flops | bytes accessed | tf_op | source)
XLA Modules:
  0.0 99.4 jit_solution(637182987848219135)
XLA Ops:
  0.6 0.0 copy-start.8
  0.7 0.7 fusion.44
  1.4 0.7 fusion.37
  4.7 0.1 concatenate.3
  4.7 0.6 broadcast_in_dim.51.bias
  6.0 0.6 broadcast_in_dim.53.take_own
  6.6 1.4 %fusion = f32[260]{0:T(512)S(1)} fusion(bf16[260,1536]{1,0:T(8,128)(2,1)} %raw_q.1), kind=kLoop, calls=%fused_computation.3 | loop fusion | flops 1197820 | bytes 799760 | tf_op jit(solution)/shard_map/reduce_sum | solution.py:317
  8.0 1.1 %fusion.7 = f32[260]{0:T(512)S(1)} fusion(bf16[260,512]{1,0:T(8,128)(2,1)} %raw_k.1), kind=kLoop, calls=%fused_computation.16 | loop fusion | flops 399100 | bytes 267280 | tf_op jit(solution)/shard_map/reduce_sum | solution.py:318
  9.1 1.1 %fusion.14 = f32[260]{0:T(512)S(1)} fusion(bf16[260,512]{1,0:T(8,128)(2,1)} %raw_c.1), kind=kLoop, calls=%fused_computation.23 | loop fusion | flops 399100 | bytes 267280 | tf_op jit(solution)/shard_map/reduce_sum | solution.py:319
  10.2 5.9 %psum.14 = f32[3,260]{1,0:T(4,128)S(1)} all-reduce(f32[3,260]{1,0:T(4,128)S(1)} %pad_maximum_fusion), channel_id=1, replica_groups=mesh['seq'=16,'head'=2] {'head'}, use_global_device_ids=true, to_apply=%region_3.4 | all-reduce | flops 780 | bytes 6240 | tf_op jit(solution)/shard_map/psum | solution.py:314
  16.1 0.6 fusion.42
  16.8 0.8 copy.15.q_inv
  17.6 0.8 copy.16.k_inv
  18.4 0.8 copy.17.c_inv
  19.2 0.0 copy-done.8
  19.2 0.6 broadcast_in_dim.47.q_gain
  19.8 64.2 %shard_map.136 = (bf16[260,1536]{1,0:T(8,128)(2,1)}, f32[260,1536]{1,0:T(8,128)}, f32[272,512]{1,0:T(8,128)}, bf16[272,512]{1,0:T(8,128)(2,1)}, f32[272,512]{1,0:T(8,128)}, /*index=5*/bf16[272,512]{1,0:T(8,128)(2,1)}) custom-call(bf16[260,1536]{1,0:T(8,128)(2,1)} %raw_q.1, f32[260,1]{1,0:T(8,128)} %copy.15.q_inv, f32[1,1536]{1,0:T(1,128)} %broadcast_in_dim.47.q_gain, ...), custom_call_target="tpu_custom_call" | custom-call | flops 7821066240 | bytes 16777216 | tf_op jit(solution)/shard_map/pallas_call | solution.py:272
  84.0 0.0 copy-start
  84.0 0.0 copy-done.2
  84.0 0.0 copy-done.3
  84.0 0.0 copy-done.9
  84.1 1.5 %fusion.8 = (f32[260]{0:T(512)S(1)}, f32[260]{0:T(512)S(1)}) fusion(bf16[260,512]{1,0:T(8,128)(2,1)S(1)} %copy-done.3, f32[272,512]{1,0:T(8,128)} %get-tuple-element.14, f32[512]{0:T(512)S(1)} %copy-done.9, bf16[260,512]{1,0:T(8,128)(2,1)S(1)} %copy-done.2, f32[272,512]{1,0:T(8,128)} %get-tuple-element.15), kind=kLoop, calls=%fused_computation.17 | loop fusion | flops 1064440 | bytes 1601568 | tf_op jit(solution)/shard_map/reduce_sum | solution.py:364
  85.6 0.0 copy-done
  85.6 1.8 %fusion.6 = f32[260]{0:T(512)S(1)} fusion(bf16[260,1536]{1,0:T(8,128)(2,1)S(1)} %copy-done, f32[260,1536]{1,0:T(8,128)} %get-tuple-element.13, f32[1536]{0:T(1024)S(1)} %copy-done.8), kind=kLoop, calls=%fused_computation.9 | loop fusion | flops 1597180 | bytes 2403344 | tf_op jit(solution)/shard_map/reduce_sum | solution.py:363
  87.4 5.1 %psum.15 = f32[3,260]{1,0:T(4,128)S(1)} all-reduce(f32[3,260]{1,0:T(4,128)S(1)} %pad_maximum_fusion.1), channel_id=1, replica_groups=mesh['seq'=16,'head'=2] {'head'}, use_global_device_ids=true, to_apply=%region_12.13 | all-reduce | flops 780 | bytes 6240 | tf_op jit(solution)/shard_map/psum | solution.py:360
  92.6 0.0 copy-done.4
  92.6 2.2 %fusion.20 = (bf16[260,512]{1,0:T(8,128)(2,1)}, bf16[260,512]{1,0:T(8,128)(2,1)}) fusion(bf16[260,512]{1,0:T(8,128)(2,1)S(1)} %copy-done.2, f32[272,512]{1,0:T(8,128)} %get-tuple-element.15, f32[260]{0:T(512)S(1)} %get-tuple-element.21, f32[260]{0:T(512)} %get-tuple-element.18, f32[512]{0:T(512)} %param.15, f32[260]{0:T(512)S(1)} %get-tuple-element.22, ...), kind=kLoop, calls=%fused_computation.29 | loop fusion | flops 2396160 | bytes 2136128 | tf_op jit(solution)/shard_map/convert_element_type | solution.py:372
  94.9 2.2 %fusion.5 = bf16[260,1536]{1,0:T(8,128)(2,1)} fusion(bf16[260,1536]{1,0:T(8,128)(2,1)S(1)} %copy-done, f32[260,1536]{1,0:T(8,128)S(1)} %copy-done.1, f32[260]{0:T(512)S(1)} %get-tuple-element.23, f32[1536]{0:T(1024)S(1)} %copy-done.8, f32[260]{0:T(512)} %get-tuple-element.20), kind=kLoop, calls=%fused_computation.8 | loop fusion | flops 3594240 | bytes 3203104 | tf_op jit(solution)/shard_map/convert_element_type | solution.py:372
  97.1 0.7 slice.37
  97.8 0.7 slice.39
  98.5 0.0 copy-done.5
  98.5 0.9 copy.19
  (23 shorter events, 0.1 us)
Async XLA Ops:
  0.6 18.5 %copy-start.8 = (f32[1536]{0:T(1024)S(1)}, f32[1536]{0:T(1024)}, u32[]{:S(2)}) copy-start(f32[1536]{0:T(1024)} %param.14) | copy-start | bytes 18436
  19.8 64.3 %copy-start.2 = (bf16[260,512]{1,0:T(8,128)(2,1)S(1)}, bf16[260,512]{1,0:T(8,128)(2,1)}, u32[]{:S(2)}) copy-start(bf16[260,512]{1,0:T(8,128)(2,1)} %raw_c.1) | copy-start | bytes 798724
  19.8 64.3 %copy-start.3 = (bf16[260,512]{1,0:T(8,128)(2,1)S(1)}, bf16[260,512]{1,0:T(8,128)(2,1)}, u32[]{:S(2)}) copy-start(bf16[260,512]{1,0:T(8,128)(2,1)} %raw_k.1) | copy-start | bytes 798724
  19.8 64.3 %copy-start.9 = (f32[512]{0:T(512)S(1)}, f32[512]{0:T(512)}, u32[]{:S(2)}) copy-start(f32[512]{0:T(512)} %param.15) | copy-start | bytes 6148
  84.0 1.6 %copy-start = (bf16[260,1536]{1,0:T(8,128)(2,1)S(1)}, bf16[260,1536]{1,0:T(8,128)(2,1)}, u32[]{:S(2)}) copy-start(bf16[260,1536]{1,0:T(8,128)(2,1)} %raw_q.1) | copy-start | bytes 2396164
  85.6 7.0 %copy-start.4 = (f32[272,512]{1,0:T(8,128)S(1)}, f32[272,512]{1,0:T(8,128)}, u32[]{:S(2)}) copy-start(f32[272,512]{1,0:T(8,128)} %get-tuple-element.14) | copy-start | bytes 1671172
  87.4 7.4 %copy-start.1 = (f32[260,1536]{1,0:T(8,128)S(1)}, f32[260,1536]{1,0:T(8,128)}, u32[]{:S(2)}) copy-start(f32[260,1536]{1,0:T(8,128)} %get-tuple-element.13) | copy-start | bytes 4792324
  94.9 2.2 %copy-start.7 = (bf16[272,512]{1,0:T(8,128)(2,1)S(1)}, bf16[272,512]{1,0:T(8,128)(2,1)}, u32[]{:S(2)}) copy-start(bf16[272,512]{1,0:T(8,128)(2,1)} %get-tuple-element.16) | copy-start | bytes 835588
  94.9 3.0 %copy-start.6 = (bf16[272,512]{1,0:T(8,128)(2,1)S(1)}, bf16[272,512]{1,0:T(8,128)(2,1)}, u32[]{:S(2)}) copy-start(bf16[272,512]{1,0:T(8,128)(2,1)} %get-tuple-element.17) | copy-start | bytes 835588
  94.9 3.7 %copy-start.5 = (bf16[260,1536]{1,0:T(8,128)(2,1)S(1)}, bf16[260,1536]{1,0:T(8,128)(2,1)}, u32[]{:S(2)}) copy-start(bf16[260,1536]{1,0:T(8,128)(2,1)} %get-tuple-element.42) | copy-start | bytes 2396164

commit v3 on v2

--- a/solution.py
+++ b/solution.py
@@ -30,25 +30,21 @@
 
 
 def stretch_kernel(
+    window,
     raw_q,
-    q_inv,
-    q_gain,
-    grad,
-    bias,
     raw_k,
     value,
-    k_inv,
     raw_c,
     clean_value,
-    c_inv,
+    q_gain,
     key_gain,
-    take_own,
+    grad,
     out_ref,
-    dq_ref,
-    dk_ref,
-    dv_ref,
-    dck_ref,
-    dcv_ref,
+    grad_q_ref,
+    grad_k_ref,
+    grad_v_ref,
+    grad_ck_ref,
+    grad_cv_ref,
     noisy_own,
     clean_own,
     noisy_par,
@@ -64,8 +60,19 @@
     later_in,
     next_out,
     next_in,
+    q_scaled,
+    k_scaled,
+    c_scaled,
+    inner,
+    inverse_rms,
+    bias,
+    take_own,
+    stat_out,
+    stat_in,
     send_sems,
     recv_sems,
+    stat_send,
+    stat_recv,
 ):
     heads = noisy_own.shape[0]
     rows = raw_q.shape[0]
@@ -83,6 +90,75 @@
         pl.semaphore_signal(
             barrier, inc=1, device_id={"seq": peer}, device_id_type=pl.DeviceIdType.MESH
         )
+    side = lax.axis_index("head")
+    sides = lax.axis_size("head")
+    for step_by in range(1, sides):
+        pl.semaphore_signal(
+            barrier,
+            inc=1,
+            device_id={"head": (side + step_by) % sides},
+            device_id_type=pl.DeviceIdType.MESH,
+        )
+
+    def stat_copy(kind, step_by):
+        return pltpu.make_async_remote_copy(
+            src_ref=stat_out.at[kind],
+            dst_ref=stat_in.at[kind, step_by - 1],
+            send_sem=stat_send.at[kind, step_by - 1],
+            recv_sem=stat_recv.at[kind, step_by - 1],
+            device_id={"head": (side + step_by) % sides},
+            device_id_type=pl.DeviceIdType.MESH,
+        )
+
+    def share(kind, columns):
+        lane = lax.broadcasted_iota(jnp.int32, (rows, HEAD_SIZE), 1)
+        packed = jnp.zeros((rows, HEAD_SIZE), jnp.float32)
+        for at, column in enumerate(columns):
+            packed = jnp.where(lane == at, column, packed)
+        stat_out[kind, :rows] = packed
+        for step_by in range(1, sides):
+            stat_copy(kind, step_by).start()
+
+    def shared(kind):
+        total = stat_out[kind]
+        for step_by in range(1, sides):
+            stat_copy(kind, step_by).wait_recv()
+            total = total + stat_in[kind, step_by - 1]
+        return total[:rows]
+
+    def square_sum(ref):
+        total = jnp.zeros((rows, HEAD_SIZE), jnp.float32)
+        for first in range(0, ref.shape[1], HEAD_SIZE):
+            full = ref[:, first : first + HEAD_SIZE].astype(jnp.float32)
+            total = total + full * full
+        return jnp.sum(total, axis=1, keepdims=True)
+
+    q_width = HQ * HEAD_SIZE
+    key_width = KEY_VALUE_HEADS * HEAD_SIZE
+    stat_out[...] = jnp.zeros_like(stat_out)
+    square_sums = [square_sum(ref) for ref in (raw_q, raw_k, raw_c)]
+    pl.semaphore_wait(barrier, len(peers) + sides - 1)
+    share(0, square_sums)
+
+    stretch_id = here // 2
+    later_id = (stretch_id + 2) % window.shape[0]
+    first_entry, second_entry = window[stretch_id, 0], window[stretch_id, 1]
+    high = jnp.maximum(first_entry, second_entry)
+    low = jnp.minimum(first_entry, second_entry)
+    later_low = jnp.minimum(window[later_id, 0], window[later_id, 1])
+    own_id = jnp.full((1, HEAD_SIZE), stretch_id, jnp.int32)
+    take_own[...] = jnp.where(jnp.full((1, HEAD_SIZE), later_low) == own_id, 1.0, 0.0)
+    lane = lax.broadcasted_iota(jnp.int32, bias.shape, 1)
+    held = jnp.zeros(bias.shape, jnp.float32)
+    for index in range(PIECES):
+        at = index * piece_rows
+        inside = jnp.where((lane >= at) & (lane < at + rows), 1.0, 0.0)
+        if index >= 2:
+            entry = jnp.full(bias.shape, high if index < 4 else low)
+            inside = jnp.where(entry >= 0, inside, 0.0)
+        held = held + inside
+    bias[...] = jnp.where(held > 0.0, 0.0, NEG_FILL)
+    inner[...] = jnp.zeros_like(inner)
 
     def copy(kind, head, src, dst, target):
         return pltpu.make_async_remote_copy(
@@ -115,18 +191,20 @@
 
     noisy_own[...] = jnp.zeros_like(noisy_own)
     clean_own[...] = jnp.zeros_like(clean_own)
+    totals = shared(0)
+    for at, width in enumerate((q_width, key_width, key_width)):
+        mean = totals[:, at : at + 1] * (1.0 / width)
+        inverse_rms[at] = jnp.broadcast_to(lax.rsqrt(mean + EPSILON), (rows, HEAD_SIZE))
     for h in range(heads):
         cols = slice(h * HEAD_SIZE, (h + 1) * HEAD_SIZE)
         gain_row = key_gain[:, cols]
-        clean_own[h, 0, :rows] = (raw_c[:, cols].astype(jnp.float32) * c_inv[...] * gain_row).astype(
+        clean_own[h, 0, :rows] = (raw_c[:, cols].astype(jnp.float32) * inverse_rms[2] * gain_row).astype(
             jnp.bfloat16
         )
         clean_own[h, 1, :rows] = clean_value[:, cols]
-        if h == 0:
-            pl.semaphore_wait(barrier, len(peers))
         if h < 2:
             clean_next(h).start()
-        noisy_own[h, 0, :rows] = (raw_k[:, cols].astype(jnp.float32) * k_inv[...] * gain_row).astype(
+        noisy_own[h, 0, :rows] = (raw_k[:, cols].astype(jnp.float32) * inverse_rms[1] * gain_row).astype(
             jnp.bfloat16
         )
         noisy_own[h, 1, :rows] = value[:, cols]
@@ -150,8 +228,10 @@
         grad_later(h).start()
         cols = pl.ds(pl.multiple_of(h * HEAD_SIZE, HEAD_SIZE), HEAD_SIZE)
         total = grad_own[h, 0] + grad_in[h, 0].astype(jnp.float32)
-        dk_ref[:, cols] = total[0]
-        dv_ref[:, cols] = total[1].astype(jnp.bfloat16)
+        scaled = total[0, :rows] * key_gain[:, cols]
+        k_scaled[:, cols] = scaled
+        inner[1] += scaled * raw_k[:, cols].astype(jnp.float32)
+        grad_v_ref[:, cols] = total[1, :rows].astype(jnp.bfloat16)
         grad_own[h, 1] = grad_own[h, 1] + grad_in[h, 1].astype(jnp.float32)
 
     def pass_later(h):
@@ -168,8 +248,18 @@
             own, later_in[h].astype(jnp.float32), 0.0
         )
         cols = pl.ds(pl.multiple_of(h * HEAD_SIZE, HEAD_SIZE), HEAD_SIZE)
-        dck_ref[:, cols] = total[0]
-        dcv_ref[:, cols] = total[1].astype(jnp.bfloat16)
+        scaled = total[0, :rows] * key_gain[:, cols]
+        c_scaled[:, cols] = scaled
+        inner[2] += scaled * raw_c[:, cols].astype(jnp.float32)
+        grad_cv_ref[:, cols] = total[1, :rows].astype(jnp.bfloat16)
+
+    def norm_grad(ref, raw, scaled, at, inner_sum, width):
+        inv = inverse_rms[at]
+        factor = inv * inv * inv * (inner_sum * (1.0 / width))
+        for first in range(0, ref.shape[1], HEAD_SIZE):
+            cols = slice(first, first + HEAD_SIZE)
+            full = raw[:, cols].astype(jnp.float32)
+            ref[:, cols] = (inv * scaled[:, cols] - full * factor).astype(ref.dtype)
 
     for h in range(min(2, heads)):
         pass_clean(h)
@@ -190,7 +280,7 @@
             first = pl.multiple_of((h * GROUP + member) * HEAD_SIZE, HEAD_SIZE)
             cols = pl.ds(first, HEAD_SIZE)
             gain_row = q_gain[:, cols] * (scale * LOG2E)
-            query = (raw_q[:, cols].astype(jnp.float32) * q_inv[...] * gain_row).astype(
+            query = (raw_q[:, cols].astype(jnp.float32) * inverse_rms[0] * gain_row).astype(
                 jnp.bfloat16
             )
             scores = lax.dot_general(
@@ -210,7 +300,10 @@
                 grad_low, values, (((1,), (1,)), ((), ())), preferred_element_type=jnp.float32
             )
             dscores = (weights * (dprobs - delta)).astype(jnp.bfloat16)
-            dq_ref[:, cols] = jnp.dot(dscores, keys, preferred_element_type=jnp.float32) * scale
+            dq = jnp.dot(dscores, keys, preferred_element_type=jnp.float32)
+            scaled = dq * (q_gain[:, cols] * scale)
+            q_scaled[:, cols] = scaled
+            inner[0] += scaled * raw_q[:, cols].astype(jnp.float32)
             dk_total += lax.dot_general(
                 dscores, query, (((0,), (0,)), ((), ())), preferred_element_type=jnp.float32
             )
@@ -236,51 +329,55 @@
 
     lax.fori_loop(0, heads, step, 0)
     pass_grads(heads - 1)
+    share(1, [jnp.sum(inner[at], axis=1, keepdims=True) for at in range(2)])
     for h in range(max(heads - 2, 0), heads):
         pass_later(h)
+    totals = shared(1)
+    norm_grad(grad_q_ref, raw_q, q_scaled, 0, totals[:, 0:1], q_width)
+    norm_grad(grad_k_ref, raw_k, k_scaled, 1, totals[:, 1:2], key_width)
     for h in range(heads):
         finish(h)
+    share(2, [jnp.sum(inner[2], axis=1, keepdims=True)])
+    totals = shared(2)
+    norm_grad(grad_ck_ref, raw_c, c_scaled, 2, totals[:, 0:1], key_width)
     for kind in kinds:
         for h in range(heads):
             kind(h).wait_send()
-
-
-def attend(raw_q, q_inv, q_gain, grad, bias, raw_k, value, k_inv, raw_c, clean_value, c_inv, key_gain, take_own):
-    rows, width = raw_q.shape
-    heads = raw_k.shape[1] // HEAD_SIZE
+    for kind in range(3):
+        for step_by in range(1, sides):
+            stat_copy(kind, step_by).wait_send()
+
+
+def on_device(
+    noisy_q, noisy_k, noisy_value, clean_k, clean_value, q_gain, key_norm_gain, out_grad, window
+):
+    rows, width = noisy_q.shape
+    assert STRETCH == 2 * rows
+    heads = noisy_k.shape[1] // HEAD_SIZE
+    sides = lax.axis_size("head")
     piece_rows = padded_rows(rows)
     key_rows = PIECES * piece_rows
     piece = pltpu.VMEM((heads, 2, piece_rows, HEAD_SIZE), jnp.bfloat16)
     triple = (heads, 3, 2, piece_rows, HEAD_SIZE)
-    key_out = (piece_rows, heads * HEAD_SIZE)
     args = (
-        raw_q,
-        q_inv,
+        window,
+        noisy_q,
+        noisy_k,
+        noisy_value,
+        clean_k,
+        clean_value,
         q_gain[None, :],
-        grad,
-        bias,
-        raw_k,
-        value,
-        k_inv,
-        raw_c,
-        clean_value,
-        c_inv,
-        key_gain[None, :],
-        take_own,
+        key_norm_gain[None, :],
+        out_grad,
     )
     vmem = pl.BlockSpec(memory_space=pltpu.VMEM)
+    wide = jax.ShapeDtypeStruct(noisy_q.shape, jnp.bfloat16)
+    narrow = jax.ShapeDtypeStruct(noisy_k.shape, jnp.bfloat16)
     return pl.pallas_call(
         stretch_kernel,
-        in_specs=[vmem] * len(args),
+        in_specs=[pl.BlockSpec(memory_space=pltpu.SMEM)] + [vmem] * (len(args) - 1),
         out_specs=[vmem] * 6,
-        out_shape=[
-            jax.ShapeDtypeStruct((rows, width), jnp.bfloat16),
-            jax.ShapeDtypeStruct((rows, width), jnp.float32),
-            jax.ShapeDtypeStruct(key_out, jnp.float32),
-            jax.ShapeDtypeStruct(key_out, jnp.bfloat16),
-            jax.ShapeDtypeStruct(key_out, jnp.float32),
-            jax.ShapeDtypeStruct(key_out, jnp.bfloat16),
-        ],
+        out_shape=[wide, wide, narrow, narrow, narrow, narrow],
         scratch_shapes=[piece] * 8
         + [
             pltpu.VMEM(triple, jnp.float32),
@@ -288,7 +385,21 @@
             pltpu.VMEM(triple, jnp.bfloat16),
         ]
         + [piece] * 4
-        + [pltpu.SemaphoreType.DMA((8, heads)), pltpu.SemaphoreType.DMA((8, heads))],
+        + [
+            pltpu.VMEM(noisy_q.shape, jnp.float32),
+            pltpu.VMEM(noisy_k.shape, jnp.float32),
+            pltpu.VMEM(noisy_k.shape, jnp.float32),
+            pltpu.VMEM((3, rows, HEAD_SIZE), jnp.float32),
+            pltpu.VMEM((3, rows, HEAD_SIZE), jnp.float32),
+            pltpu.VMEM((1, key_rows), jnp.float32),
+            pltpu.VMEM((1, HEAD_SIZE), jnp.float32),
+            pltpu.VMEM((3, piece_rows, HEAD_SIZE), jnp.float32),
+            pltpu.VMEM((3, max(sides - 1, 1), piece_rows, HEAD_SIZE), jnp.float32),
+            pltpu.SemaphoreType.DMA((8, heads)),
+            pltpu.SemaphoreType.DMA((8, heads)),
+            pltpu.SemaphoreType.DMA((3, max(sides - 1, 1))),
+            pltpu.SemaphoreType.DMA((3, max(sides - 1, 1))),
+        ],
         compiler_params=pltpu.CompilerParams(
             collective_id=0, has_side_effects=True, vmem_limit_bytes=58 * 1024 * 1024
         ),
@@ -300,85 +411,6 @@
     )(*args)
 
 
-def on_device(
-    noisy_q, noisy_k, noisy_value, clean_k, clean_value, q_gain, key_norm_gain, out_grad, window
-):
-    rows = noisy_q.shape[0]
-    span = STRETCH // rows
-    assert span == 2
-    piece_rows = padded_rows(rows)
-    stretch_id = lax.axis_index("seq") // span
-    q_full = noisy_q.astype(jnp.float32)
-    k_full = noisy_k.astype(jnp.float32)
-    c_full = clean_k.astype(jnp.float32)
-    totals = lax.psum(
-        jnp.stack(
-            [
-                jnp.sum(q_full * q_full, axis=1),
-                jnp.sum(k_full * k_full, axis=1),
-                jnp.sum(c_full * c_full, axis=1),
-            ]
-        ),
-        "head",
-    )
-    q_width = HQ * HEAD_SIZE
-    key_width = KEY_VALUE_HEADS * HEAD_SIZE
-    q_inv = lax.rsqrt(totals[0] / q_width + EPSILON)[:, None]
-    k_inv = lax.rsqrt(totals[1] / key_width + EPSILON)[:, None]
-    c_inv = lax.rsqrt(totals[2] / key_width + EPSILON)[:, None]
-
-    ids = jnp.arange(window.shape[0], dtype=jnp.int32)
-    low = jnp.min(window, axis=1)
-    high = jnp.max(window, axis=1)
-    pick = lambda table, at: jnp.sum(jnp.where(ids == at, table, 0))
-    has_prev = pick(high, stretch_id) >= 0
-    has_other = (pick(low, stretch_id) >= 0) & (pick(low, stretch_id) < pick(high, stretch_id))
-    later_takes_own = pick(low, stretch_id + 2) == stretch_id
-
-    real = jnp.arange(piece_rows) < rows
-    flags = [True, True, has_prev, has_prev, has_other, has_other]
-    bias = jnp.concatenate([jnp.where(real & flag, 0.0, NEG_FILL) for flag in flags])
-    attn_out, dq_norm, dk_norm, grad_v, dc_norm, grad_clean_v = attend(
-        noisy_q,
-        q_inv,
-        q_gain,
-        out_grad,
-        bias[None, :].astype(jnp.float32),
-        noisy_k,
-        noisy_value,
-        k_inv,
-        clean_k,
-        clean_value,
-        c_inv,
-        key_norm_gain,
-        jnp.full((1, HEAD_SIZE), later_takes_own.astype(jnp.float32)),
-    )
-
-    q_scaled = dq_norm * q_gain[None, :]
-    k_scaled = dk_norm[:rows] * key_norm_gain[None, :]
-    c_scaled = dc_norm[:rows] * key_norm_gain[None, :]
-    inner_sum = lax.psum(
-        jnp.stack(
-            [
-                jnp.sum(q_scaled * q_full, axis=1),
-                jnp.sum(k_scaled * k_full, axis=1),
-                jnp.sum(c_scaled * c_full, axis=1),
-            ]
-        ),
-        "head",
-    )
-
-    def norm_grad(full, inv, scaled, inner, width):
-        return (inv * scaled - full * inv * inv * inv * (inner / width)[:, None]).astype(
-            jnp.bfloat16
-        )
-
-    grad_q = norm_grad(q_full, q_inv, q_scaled, inner_sum[0], q_width)
-    grad_k = norm_grad(k_full, k_inv, k_scaled, inner_sum[1], key_width)
-    grad_clean_k = norm_grad(c_full, c_inv, c_scaled, inner_sum[2], key_width)
-    return (attn_out, grad_q, grad_k, grad_v[:rows], grad_clean_k, grad_clean_v[:rows])
-
-
 def solution(mesh):
     split = P("seq", "head")
     return jax.shard_map(

time: 100 us -> 85.8 us (0.86)
  the two profiles are of different devices: /device:TPU:0 before, /device:TPU:6 now
where the time goes in v3:
time: 85.8 us; the launch traced here: 85.5 us
  Pallas kernels  75 us (87%)
  local copies, waits for them, and re-layouts  9.77 us (11%)
    pallas_call x1, Pallas kernels, on_device(): pl.pallas_call(stretch_kernel, in_specs=[pl.BlockSpec(memory_space=pltpu....  75 us
    unnamed x19, local copies, waits for them, and re-layouts  8.48 us

profile of v3, /device:TPU:6, one launch (start us, length us, event | category | flops | bytes accessed | tf_op | source)
XLA Modules:
  0.0 85.5 jit_solution(16953961635665966173)
XLA Ops:
  0.6 0.0 copy-start.5
  0.6 0.7 copy-done.5
  1.3 0.7 copy.15.window
  2.0 1.3 %broadcast_in_dim.6.q_gain = f32[1,1536]{1,0:T(1,128)} reshape(f32[1536]{0:T(1024)} %param.14) | data formatting | bytes 12288 | tf_op jit(solution)/shard_map/broadcast_in_dim | solution.py:369
  3.3 75.0 %shard_map.136 = (bf16[260,1536]{1,0:T(8,128)(2,1)}, bf16[260,1536]{1,0:T(8,128)(2,1)}, bf16[260,512]{1,0:T(8,128)(2,1)}, bf16[260,512]{1,0:T(8,128)(2,1)}, bf16...) custom-call(s32[8,2]{1,0:T(8,128)} %copy.15.window, bf16[260,1536]{1,0:T(8,128)(2,1)} %raw_q.1, bf16[260,512]{1,0:T(8,128)(2,1)} %raw_k.1, ...), custom_call_target="tpu_custom_call" | custom-call | flops 7821066240 | bytes 16777216 | tf_op jit(solution)/shard_map/pallas_call | solution.py:376
  78.3 0.0 copy-start
  78.3 2.2 %copy.22 = bf16[260,1536]{1,0:T(8,128)(2,1)} copy(bf16[260,1536]{1,0:T(8,128)(2,1)} %get-tuple-element.12) | data formatting | bytes 1597440
  80.5 0.0 copy-done
  80.5 0.0 copy-start.4
  80.5 0.9 %copy.23 = bf16[260,1536]{1,0:T(8,128)(2,1)} copy(bf16[260,1536]{1,0:T(8,128)(2,1)S(1)} %copy-done) | data formatting | bytes 1597440
  81.4 0.2 copy-done.4
  81.6 0.0 copy-start.3
  81.6 0.7 copy.24
  82.3 0.3 copy-done.3
  82.7 0.0 copy-start.2
  82.7 0.7 copy.25
  83.4 0.3 copy-done.2
  83.7 0.0 copy-start.1
  83.7 0.7 copy.26
  84.4 0.3 copy-done.1
  84.8 0.7 copy.27
Async XLA Ops:
  0.6 0.7 copy-start.5
  78.3 2.2 %copy-start = (bf16[260,1536]{1,0:T(8,128)(2,1)S(1)}, bf16[260,1536]{1,0:T(8,128)(2,1)}, u32[]{:S(2)}) copy-start(bf16[260,1536]{1,0:T(8,128)(2,1)} %get-tuple-element.13) | copy-start | bytes 2396164
  80.5 1.1 %copy-start.4 = (bf16[260,512]{1,0:T(8,128)(2,1)S(1)}, bf16[260,512]{1,0:T(8,128)(2,1)}, u32[]{:S(2)}) copy-start(bf16[260,512]{1,0:T(8,128)(2,1)} %get-tuple-element.14) | copy-start | bytes 798724
  81.6 1.1 %copy-start.3 = (bf16[260,512]{1,0:T(8,128)(2,1)S(1)}, bf16[260,512]{1,0:T(8,128)(2,1)}, u32[]{:S(2)}) copy-start(bf16[260,512]{1,0:T(8,128)(2,1)} %get-tuple-element.15) | copy-start | bytes 798724
  82.7 1.1 %copy-start.2 = (bf16[260,512]{1,0:T(8,128)(2,1)S(1)}, bf16[260,512]{1,0:T(8,128)(2,1)}, u32[]{:S(2)}) copy-start(bf16[260,512]{1,0:T(8,128)(2,1)} %get-tuple-element.16) | copy-start | bytes 798724
  83.7 1.1 %copy-start.1 = (bf16[260,512]{1,0:T(8,128)(2,1)S(1)}, bf16[260,512]{1,0:T(8,128)(2,1)}, u32[]{:S(2)}) copy-start(bf16[260,512]{1,0:T(8,128)(2,1)} %get-tuple-element.17) | copy-start | bytes 798724

commit v4 on v3

--- a/solution.py
+++ b/solution.py
@@ -136,6 +136,10 @@
     q_width = HQ * HEAD_SIZE
     key_width = KEY_VALUE_HEADS * HEAD_SIZE
     stat_out[...] = jnp.zeros_like(stat_out)
+    noisy_own[...] = jnp.zeros_like(noisy_own)
+    clean_own[...] = jnp.zeros_like(clean_own)
+    for h in range(heads):
+        clean_own[h, 1, :rows] = clean_value[:, h * HEAD_SIZE : (h + 1) * HEAD_SIZE]
     square_sums = [square_sum(ref) for ref in (raw_q, raw_k, raw_c)]
     pl.semaphore_wait(barrier, len(peers) + sides - 1)
     share(0, square_sums)
@@ -160,17 +164,19 @@
     bias[...] = jnp.where(held > 0.0, 0.0, NEG_FILL)
     inner[...] = jnp.zeros_like(inner)
 
-    def copy(kind, head, src, dst, target):
+    def copy(kind, head, src, dst, target, part=None):
+        where = head if part is None else (head, part)
         return pltpu.make_async_remote_copy(
-            src_ref=src.at[head],
-            dst_ref=dst.at[head],
+            src_ref=src.at[where],
+            dst_ref=dst.at[where],
             send_sem=send_sems.at[kind, head],
             recv_sem=recv_sems.at[kind, head],
             device_id={"seq": target},
             device_id_type=pl.DeviceIdType.MESH,
         )
 
-    clean_next = lambda h: copy(0, h, clean_own, prev_own, ahead(1))
+    key_next = lambda h: copy(0, h, clean_own, prev_own, ahead(1), 0)
+    value_next = lambda h: copy(8, h, clean_own, prev_own, ahead(1), 1)
     noisy_pair = lambda h: copy(1, h, noisy_own, noisy_par, partner)
     prev_pair = lambda h: copy(2, h, prev_own, prev_par, partner)
     clean_later = lambda h: copy(3, h, relay, other_own, ahead(2))
@@ -178,32 +184,45 @@
     grad_pair = lambda h: copy(5, h, grad_out, grad_in, partner)
     grad_later = lambda h: copy(6, h, later_out, later_in, back(2))
     grad_next = lambda h: copy(7, h, next_out, next_in, back(1))
-    kinds = (
-        clean_next,
-        noisy_pair,
-        prev_pair,
-        clean_later,
-        other_pair,
-        grad_pair,
-        grad_later,
-        grad_next,
-    )
-
-    noisy_own[...] = jnp.zeros_like(noisy_own)
-    clean_own[...] = jnp.zeros_like(clean_own)
+    stretches = window.shape[0]
+    has_prev = stretch_id >= 1
+    has_other = stretch_id >= 2
+    has_next = stretch_id + 1 < stretches
+    has_later = stretch_id + 2 < stretches
+
+    @pl.when(has_next)
+    def _():
+        for h in range(min(2, heads)):
+            value_next(h).start()
+
+    @pl.when(jnp.logical_not(has_prev))
+    def _():
+        prev_own[...] = jnp.zeros_like(prev_own)
+
+    @pl.when(jnp.logical_not(has_other))
+    def _():
+        other_own[...] = jnp.zeros_like(other_own)
+
+    @pl.when(jnp.logical_not(has_next))
+    def _():
+        next_in[...] = jnp.zeros_like(next_in)
+
+    @pl.when(jnp.logical_not(has_later))
+    def _():
+        later_in[...] = jnp.zeros_like(later_in)
+
     totals = shared(0)
     for at, width in enumerate((q_width, key_width, key_width)):
         mean = totals[:, at : at + 1] * (1.0 / width)
         inverse_rms[at] = jnp.broadcast_to(lax.rsqrt(mean + EPSILON), (rows, HEAD_SIZE))
     for h in range(heads):
         cols = slice(h * HEAD_SIZE, (h + 1) * HEAD_SIZE)
-        gain_row = key_gain[:, cols]
+        gain_row = key_gain[cols].reshape(1, HEAD_SIZE)
         clean_own[h, 0, :rows] = (raw_c[:, cols].astype(jnp.float32) * inverse_rms[2] * gain_row).astype(
             jnp.bfloat16
         )
-        clean_own[h, 1, :rows] = clean_value[:, cols]
         if h < 2:
-            clean_next(h).start()
+            pl.when(has_next)(key_next(h).start)
         noisy_own[h, 0, :rows] = (raw_k[:, cols].astype(jnp.float32) * inverse_rms[1] * gain_row).astype(
             jnp.bfloat16
         )
@@ -211,44 +230,48 @@
         noisy_pair(h).start()
 
     def pass_clean(h):
-        clean_next(h).wait_recv()
+        @pl.when(has_prev)
+        def _():
+            value_next(h).wait_recv()
+            key_next(h).wait_recv()
+
         prev_pair(h).start()
         own = clean_own[h].astype(jnp.float32)
         prev = prev_own[h].astype(jnp.float32)
         relay[h] = jnp.where(take_own[...] > 0.0, own, prev).astype(jnp.bfloat16)
-        clean_later(h).start()
+        pl.when(has_later)(clean_later(h).start)
 
     def pass_other(h):
-        clean_later(h).wait_recv()
+        pl.when(has_other)(clean_later(h).wait_recv)
         other_pair(h).start()
 
     def pass_grads(h):
         grad_pair(h).wait_recv()
         later_out[h] = (grad_own[h, 2] + grad_in[h, 2].astype(jnp.float32)).astype(jnp.bfloat16)
-        grad_later(h).start()
+        pl.when(has_other)(grad_later(h).start)
         cols = pl.ds(pl.multiple_of(h * HEAD_SIZE, HEAD_SIZE), HEAD_SIZE)
         total = grad_own[h, 0] + grad_in[h, 0].astype(jnp.float32)
-        scaled = total[0, :rows] * key_gain[:, cols]
+        scaled = total[0, :rows] * key_gain[cols].reshape(1, HEAD_SIZE)
         k_scaled[:, cols] = scaled
         inner[1] += scaled * raw_k[:, cols].astype(jnp.float32)
         grad_v_ref[:, cols] = total[1, :rows].astype(jnp.bfloat16)
         grad_own[h, 1] = grad_own[h, 1] + grad_in[h, 1].astype(jnp.float32)
 
     def pass_later(h):
-        grad_later(h).wait_recv()
+        pl.when(has_later)(grad_later(h).wait_recv)
         arrived = later_in[h].astype(jnp.float32)
         own = take_own[...] > 0.0
         next_out[h] = (grad_own[h, 1] + jnp.where(own, 0.0, arrived)).astype(jnp.bfloat16)
-        grad_next(h).start()
+        pl.when(has_prev)(grad_next(h).start)
 
     def finish(h):
-        grad_next(h).wait_recv()
+        pl.when(has_next)(grad_next(h).wait_recv)
         own = take_own[...] > 0.0
         total = next_in[h].astype(jnp.float32) + jnp.where(
             own, later_in[h].astype(jnp.float32), 0.0
         )
         cols = pl.ds(pl.multiple_of(h * HEAD_SIZE, HEAD_SIZE), HEAD_SIZE)
-        scaled = total[0, :rows] * key_gain[:, cols]
+        scaled = total[0, :rows] * key_gain[cols].reshape(1, HEAD_SIZE)
         c_scaled[:, cols] = scaled
         inner[2] += scaled * raw_c[:, cols].astype(jnp.float32)
         grad_cv_ref[:, cols] = total[1, :rows].astype(jnp.bfloat16)
@@ -264,7 +287,8 @@
     for h in range(min(2, heads)):
         pass_clean(h)
         if h + 2 < heads:
-            clean_next(h + 2).start()
+            pl.when(has_next)(value_next(h + 2).start)
+            pl.when(has_next)(key_next(h + 2).start)
     pass_other(0)
 
     own_par = (noisy_own, noisy_par, prev_own, prev_par, other_own, other_par)
@@ -279,7 +303,7 @@
         for member in range(GROUP):
             first = pl.multiple_of((h * GROUP + member) * HEAD_SIZE, HEAD_SIZE)
             cols = pl.ds(first, HEAD_SIZE)
-            gain_row = q_gain[:, cols] * (scale * LOG2E)
+            gain_row = q_gain[cols].reshape(1, HEAD_SIZE) * (scale * LOG2E)
             query = (raw_q[:, cols].astype(jnp.float32) * inverse_rms[0] * gain_row).astype(
                 jnp.bfloat16
             )
@@ -301,7 +325,7 @@
             )
             dscores = (weights * (dprobs - delta)).astype(jnp.bfloat16)
             dq = jnp.dot(dscores, keys, preferred_element_type=jnp.float32)
-            scaled = dq * (q_gain[:, cols] * scale)
+            scaled = dq * (q_gain[cols].reshape(1, HEAD_SIZE) * scale)
             q_scaled[:, cols] = scaled
             inner[0] += scaled * raw_q[:, cols].astype(jnp.float32)
             dk_total += lax.dot_general(
@@ -340,12 +364,35 @@
     share(2, [jnp.sum(inner[2], axis=1, keepdims=True)])
     totals = shared(2)
     norm_grad(grad_ck_ref, raw_c, c_scaled, 2, totals[:, 0:1], key_width)
-    for kind in kinds:
-        for h in range(heads):
+    for h in range(heads):
+        for kind in (noisy_pair, prev_pair, other_pair, grad_pair):
             kind(h).wait_send()
+
+    def wait_sends(held, kinds):
+        @pl.when(held)
+        def _():
+            for h in range(heads):
+                for kind in kinds:
+                    kind(h).wait_send()
+
+    wait_sends(has_next, (value_next, key_next))
+    wait_sends(has_later, (clean_later,))
+    wait_sends(has_other, (grad_later,))
+    wait_sends(has_prev, (grad_next,))
     for kind in range(3):
         for step_by in range(1, sides):
             stat_copy(kind, step_by).wait_send()
+
+
+def hand_over_kernel(*refs):
+    sems = refs[12]
+    copies = [
+        pltpu.make_async_copy(refs[at], refs[6 + at], sems.at[at]) for at in range(6)
+    ]
+    for copy in copies:
+        copy.start()
+    for copy in copies:
+        copy.wait()
 
 
 def on_device(
@@ -366,14 +413,14 @@
         noisy_value,
         clean_k,
         clean_value,
-        q_gain[None, :],
-        key_norm_gain[None, :],
+        q_gain,
+        key_norm_gain,
         out_grad,
     )
     vmem = pl.BlockSpec(memory_space=pltpu.VMEM)
     wide = jax.ShapeDtypeStruct(noisy_q.shape, jnp.bfloat16)
     narrow = jax.ShapeDtypeStruct(noisy_k.shape, jnp.bfloat16)
-    return pl.pallas_call(
+    results = pl.pallas_call(
         stretch_kernel,
         in_specs=[pl.BlockSpec(memory_space=pltpu.SMEM)] + [vmem] * (len(args) - 1),
         out_specs=[vmem] * 6,
@@ -395,8 +442,8 @@
             pltpu.VMEM((1, HEAD_SIZE), jnp.float32),
             pltpu.VMEM((3, piece_rows, HEAD_SIZE), jnp.float32),
             pltpu.VMEM((3, max(sides - 1, 1), piece_rows, HEAD_SIZE), jnp.float32),
-            pltpu.SemaphoreType.DMA((8, heads)),
-            pltpu.SemaphoreType.DMA((8, heads)),
+            pltpu.SemaphoreType.DMA((9, heads)),
+            pltpu.SemaphoreType.DMA((9, heads)),
             pltpu.SemaphoreType.DMA((3, max(sides - 1, 1))),
             pltpu.SemaphoreType.DMA((3, max(sides - 1, 1))),
         ],
@@ -409,6 +456,14 @@
             transcendentals=rows * GROUP * heads * key_rows,
         ),
     )(*args)
+    in_place = pl.BlockSpec(memory_space=pl.ANY)
+    return pl.pallas_call(
+        hand_over_kernel,
+        in_specs=[in_place] * 6,
+        out_specs=[in_place] * 6,
+        out_shape=[wide, wide, narrow, narrow, narrow, narrow],
+        scratch_shapes=[pltpu.SemaphoreType.DMA((6,))],
+    )(*results)
 
 
 def solution(mesh):

time: 85.8 us -> 159 us (1.85)
  the two profiles are of different devices: /device:TPU:6 before, /device:TPU:0 now
where the time goes in v4:
time: 159 us; the launch traced here: 157 us
  Pallas kernels  155 us (97%)
    pallas_call x1, Pallas kernels, on_device(): pl.pallas_call(hand_over_kernel, in_specs=[in_place] * 6, out_specs=[in_p...  83.1 us
    pallas_call x1, Pallas kernels, on_device(): pl.pallas_call(stretch_kernel, in_specs=[pl.BlockSpec(memory_space=pltpu....  71.5 us

profile of v4, /device:TPU:0, one launch (start us, length us, event | category | flops | bytes accessed | tf_op | source)
XLA Modules:
  0.0 156.5 jit_solution(16143276217157434015)
XLA Ops:
  0.6 1.3 copy.15.window
  2.0 71.5 %shard_map.136 = (bf16[260,1536]{1,0:T(8,128)(2,1)}, bf16[260,1536]{1,0:T(8,128)(2,1)}, bf16[260,512]{1,0:T(8,128)(2,1)}, bf16[260,512]{1,0:T(8,128)(2,1)}, bf16...) custom-call(s32[8,2]{1,0:T(8,128)} %copy.15.window, bf16[260,1536]{1,0:T(8,128)(2,1)} %raw_q.1, bf16[260,512]{1,0:T(8,128)(2,1)} %raw_k.1, ...), custom_call_target="tpu_custom_call" | custom-call | flops 7821066240 | bytes 16777216 | tf_op jit(solution)/shard_map/pallas_call | solution.py:423
  73.5 83.1 %shard_map.137 = (bf16[260,1536]{1,0:T(8,128)(2,1)}, bf16[260,1536]{1,0:T(8,128)(2,1)}, bf16[260,512]{1,0:T(8,128)(2,1)}, bf16[260,512]{1,0:T(8,128)(2,1)}, bf16...) custom-call(bf16[260,1536]{1,0:T(8,128)(2,1)} %get-tuple-element.12.refs_0_, bf16[260,1536]{1,0:T(8,128)(2,1)} %get-tuple-element.13.refs_1_, ...), custom_call_target="tpu_custom_call" | custom-call | tf_op jit(solution)/shard_map/pallas_call | solution.py:460

commit v5 on v4

--- a/solution.py
+++ b/solution.py
@@ -67,6 +67,10 @@
     inverse_rms,
     bias,
     take_own,
+    all_dscores,
+    all_weights,
+    all_queries,
+    all_grads,
     stat_out,
     stat_in,
     send_sems,
@@ -163,6 +167,14 @@
         held = held + inside
     bias[...] = jnp.where(held > 0.0, 0.0, NEG_FILL)
     inner[...] = jnp.zeros_like(inner)
+    key_rows = bias.shape[1]
+    for ref in (all_dscores, all_weights, all_queries, all_grads):
+        for member in range(GROUP):
+            end = (member + 1) * piece_rows
+            ref[end - 16 : end] = jnp.zeros((16, ref.shape[1]), jnp.bfloat16)
+    for ref in (all_dscores, all_weights):
+        spare = ref.shape[1] - HEAD_SIZE
+        ref[:, spare:] = jnp.zeros((ref.shape[0], HEAD_SIZE), jnp.bfloat16)
 
     def copy(kind, head, src, dst, target, part=None):
         where = head if part is None else (head, part)
@@ -299,7 +311,6 @@
         other_pair(h).wait_recv()
         keys = key_pieces(own_par, h, 0)
         values = key_pieces(own_par, h, 1)
-        dk_total, dv_total = 0.0, 0.0
         for member in range(GROUP):
             first = pl.multiple_of((h * GROUP + member) * HEAD_SIZE, HEAD_SIZE)
             cols = pl.ds(first, HEAD_SIZE)
@@ -323,24 +334,30 @@
             dprobs = lax.dot_general(
                 grad_low, values, (((1,), (1,)), ((), ())), preferred_element_type=jnp.float32
             )
-            dscores = (weights * (dprobs - delta)).astype(jnp.bfloat16)
+            dscores = weights_low * (dprobs - delta).astype(jnp.bfloat16)
             dq = jnp.dot(dscores, keys, preferred_element_type=jnp.float32)
             scaled = dq * (q_gain[cols].reshape(1, HEAD_SIZE) * scale)
             q_scaled[:, cols] = scaled
             inner[0] += scaled * raw_q[:, cols].astype(jnp.float32)
-            dk_total += lax.dot_general(
-                dscores, query, (((0,), (0,)), ((), ())), preferred_element_type=jnp.float32
-            )
-            dv_total += lax.dot_general(
-                weights_low, grad_low, (((0,), (0,)), ((), ())), preferred_element_type=jnp.float32
-            )
+            span = slice(member * piece_rows, member * piece_rows + rows)
+            all_dscores[span, :key_rows] = dscores
+            all_weights[span, :key_rows] = weights_low
+            all_queries[span] = query
+            all_grads[span] = grad_low
             if member == 0:
                 pl.when(h + 2 < heads)(lambda: pass_clean(h + 2))
                 pl.when(h >= 1)(lambda: pass_grads(h - 1))
-            if member == 1:
                 pl.when(h + 1 < heads)(lambda: pass_other(h + 1))
                 pl.when(h >= 2)(lambda: pass_later(h - 2))
-        dk_total = dk_total * (1.0 / LOG2E)
+
+        def key_sums(small, large):
+            across = lax.dot_general(
+                small[...], large[...], (((0,), (0,)), ((), ())), preferred_element_type=jnp.float32
+            )
+            return across.T
+
+        dk_total = key_sums(all_queries, all_dscores) * (1.0 / LOG2E)
+        dv_total = key_sums(all_grads, all_weights)
         for index in range(PIECES // 2):
             for part, total in enumerate((dk_total, dv_total)):
                 at = 2 * index * piece_rows
@@ -385,14 +402,8 @@
 
 
 def hand_over_kernel(*refs):
-    sems = refs[12]
-    copies = [
-        pltpu.make_async_copy(refs[at], refs[6 + at], sems.at[at]) for at in range(6)
-    ]
-    for copy in copies:
-        copy.start()
-    for copy in copies:
-        copy.wait()
+    for at in range(6):
+        refs[6 + at][...] = refs[at][...]
 
 
 def on_device(
@@ -404,6 +415,7 @@
     sides = lax.axis_size("head")
     piece_rows = padded_rows(rows)
     key_rows = PIECES * piece_rows
+    stacked = (GROUP * piece_rows, -(-key_rows // HEAD_SIZE) * HEAD_SIZE)
     piece = pltpu.VMEM((heads, 2, piece_rows, HEAD_SIZE), jnp.bfloat16)
     triple = (heads, 3, 2, piece_rows, HEAD_SIZE)
     args = (
@@ -440,6 +452,10 @@
             pltpu.VMEM((3, rows, HEAD_SIZE), jnp.float32),
             pltpu.VMEM((1, key_rows), jnp.float32),
             pltpu.VMEM((1, HEAD_SIZE), jnp.float32),
+            pltpu.VMEM(stacked, jnp.bfloat16),
+            pltpu.VMEM(stacked, jnp.bfloat16),
+            pltpu.VMEM((stacked[0], HEAD_SIZE), jnp.bfloat16),
+            pltpu.VMEM((stacked[0], HEAD_SIZE), jnp.bfloat16),
             pltpu.VMEM((3, piece_rows, HEAD_SIZE), jnp.float32),
             pltpu.VMEM((3, max(sides - 1, 1), piece_rows, HEAD_SIZE), jnp.float32),
             pltpu.SemaphoreType.DMA((9, heads)),
@@ -456,13 +472,15 @@
             transcendentals=rows * GROUP * heads * key_rows,
         ),
     )(*args)
-    in_place = pl.BlockSpec(memory_space=pl.ANY)
+    blocks = [
+        pl.BlockSpec((rows, array.shape[1] // heads), lambda j: (0, j)) for array in results
+    ]
     return pl.pallas_call(
         hand_over_kernel,
-        in_specs=[in_place] * 6,
-        out_specs=[in_place] * 6,
+        grid=(heads,),
+        in_specs=blocks,
+        out_specs=blocks,
         out_shape=[wide, wide, narrow, narrow, narrow, narrow],
-        scratch_shapes=[pltpu.SemaphoreType.DMA((6,))],
     )(*results)
 
 

time: 159 us -> 77.2 us (0.49); the launches traced: 157 us -> 77 us
  Pallas kernels: 155 us -> 75 us
    pallas_call x1, Pallas kernels: 83.1 us -> 4.11 us  [on_device(): pl.pallas_call(hand_over_kernel, grid=(heads,), in_specs=blocks, out_spec...]
where the time goes in v5:
time: 77.2 us; the launch traced here: 77 us
  Pallas kernels  75 us (97%)
  local copies, waits for them, and re-layouts  1.35 us (2%)
    pallas_call x1, Pallas kernels, on_device(): pl.pallas_call(stretch_kernel, in_specs=[pl.BlockSpec(memory_space=pltpu....  70.9 us
    pallas_call x1, Pallas kernels, on_device(): pl.pallas_call(hand_over_kernel, grid=(heads,), in_specs=blocks, out_spec...  4.11 us

profile of v5, /device:TPU:0, one launch (start us, length us, event | category | flops | bytes accessed | tf_op | source)
XLA Modules:
  0.0 77.0 jit_solution(13480821007379850489)
XLA Ops:
  0.6 1.3 %copy.15.window = s32[8,2]{1,0:T(8,128)} copy(s32[8,2]{0,1:T(2,128)} %param.17) | data formatting | bytes 128 | tf_op args[8]
  2.0 70.9 %shard_map.136 = (bf16[260,1536]{1,0:T(8,128)(2,1)}, bf16[260,1536]{1,0:T(8,128)(2,1)}, bf16[260,512]{1,0:T(8,128)(2,1)}, bf16[260,512]{1,0:T(8,128)(2,1)}, bf16...) custom-call(s32[8,2]{1,0:T(8,128)} %copy.15.window, bf16[260,1536]{1,0:T(8,128)(2,1)} %raw_q.1, bf16[260,512]{1,0:T(8,128)(2,1)} %raw_k.1, ...), custom_call_target="tpu_custom_call" | custom-call | flops 7821066240 | bytes 16777216 | tf_op jit(solution)/shard_map/pallas_call | solution.py:435
  72.9 4.1 %shard_map.137 = (bf16[260,1536]{1,0:T(8,128)(2,1)}, bf16[260,1536]{1,0:T(8,128)(2,1)}, bf16[260,512]{1,0:T(8,128)(2,1)}, bf16[260,512]{1,0:T(8,128)(2,1)}, bf16...) custom-call(bf16[260,1536]{1,0:T(8,128)(2,1)} %get-tuple-element.12.refs_0_, bf16[260,1536]{1,0:T(8,128)(2,1)} %get-tuple-element.13.refs_1_, ...), custom_call_target="tpu_custom_call" | custom-call | tf_op jit(solution)/shard_map/pallas_call | solution.py:478

commit v6 on v5

--- a/solution.py
+++ b/solution.py
@@ -176,26 +176,28 @@
         spare = ref.shape[1] - HEAD_SIZE
         ref[:, spare:] = jnp.zeros((ref.shape[0], HEAD_SIZE), jnp.bfloat16)
 
-    def copy(kind, head, src, dst, target, part=None):
-        where = head if part is None else (head, part)
+    def copy(kind, head, part, src, dst, target, piece=None):
+        where = (head, part) if piece is None else (head, piece, part)
         return pltpu.make_async_remote_copy(
             src_ref=src.at[where],
             dst_ref=dst.at[where],
-            send_sem=send_sems.at[kind, head],
-            recv_sem=recv_sems.at[kind, head],
+            send_sem=send_sems.at[kind, head, part],
+            recv_sem=recv_sems.at[kind, head, part],
             device_id={"seq": target},
             device_id_type=pl.DeviceIdType.MESH,
         )
 
-    key_next = lambda h: copy(0, h, clean_own, prev_own, ahead(1), 0)
-    value_next = lambda h: copy(8, h, clean_own, prev_own, ahead(1), 1)
-    noisy_pair = lambda h: copy(1, h, noisy_own, noisy_par, partner)
-    prev_pair = lambda h: copy(2, h, prev_own, prev_par, partner)
-    clean_later = lambda h: copy(3, h, relay, other_own, ahead(2))
-    other_pair = lambda h: copy(4, h, other_own, other_par, partner)
-    grad_pair = lambda h: copy(5, h, grad_out, grad_in, partner)
-    grad_later = lambda h: copy(6, h, later_out, later_in, back(2))
-    grad_next = lambda h: copy(7, h, next_out, next_in, back(1))
+    clean_next = lambda h, p: copy(0, h, p, clean_own, prev_own, ahead(1))
+    noisy_pair = lambda h, p: copy(1, h, p, noisy_own, noisy_par, partner)
+    prev_pair = lambda h, p: copy(2, h, p, prev_own, prev_par, partner)
+    clean_later = lambda h, p: copy(3, h, p, relay, other_own, ahead(2))
+    other_pair = lambda h, p: copy(4, h, p, other_own, other_par, partner)
+    grad_later = lambda h, p: copy(5, h, p, later_out, later_in, back(2))
+    grad_next = lambda h, p: copy(6, h, p, next_out, next_in, back(1))
+    grad_noisy = lambda h, p: copy(7, h, p, grad_out, grad_in, partner, 0)
+    grad_prev = lambda h, p: copy(8, h, p, grad_out, grad_in, partner, 1)
+    grad_other = lambda h, p: copy(9, h, p, grad_out, grad_in, partner, 2)
+
     stretches = window.shape[0]
     has_prev = stretch_id >= 1
     has_other = stretch_id >= 2
@@ -205,7 +207,7 @@
     @pl.when(has_next)
     def _():
         for h in range(min(2, heads)):
-            value_next(h).start()
+            clean_next(h, 1).start()
 
     @pl.when(jnp.logical_not(has_prev))
     def _():
@@ -234,59 +236,74 @@
             jnp.bfloat16
         )
         if h < 2:
-            pl.when(has_next)(key_next(h).start)
+            pl.when(has_next)(clean_next(h, 0).start)
         noisy_own[h, 0, :rows] = (raw_k[:, cols].astype(jnp.float32) * inverse_rms[1] * gain_row).astype(
             jnp.bfloat16
         )
         noisy_own[h, 1, :rows] = value[:, cols]
-        noisy_pair(h).start()
+        for p in range(2):
+            noisy_pair(h, p).start()
 
     def pass_clean(h):
-        @pl.when(has_prev)
-        def _():
-            value_next(h).wait_recv()
-            key_next(h).wait_recv()
-
-        prev_pair(h).start()
-        own = clean_own[h].astype(jnp.float32)
-        prev = prev_own[h].astype(jnp.float32)
-        relay[h] = jnp.where(take_own[...] > 0.0, own, prev).astype(jnp.bfloat16)
-        pl.when(has_later)(clean_later(h).start)
+        for p in (1, 0):
+            pl.when(has_prev)(clean_next(h, p).wait_recv)
+            own = clean_own[h, p].astype(jnp.float32)
+            prev = prev_own[h, p].astype(jnp.float32)
+            relay[h, p] = jnp.where(take_own[...] > 0.0, own, prev).astype(jnp.bfloat16)
+            pl.when(has_later)(clean_later(h, p).start)
+            prev_pair(h, p).start()
 
     def pass_other(h):
-        pl.when(has_other)(clean_later(h).wait_recv)
-        other_pair(h).start()
+        for p in (1, 0):
+            pl.when(has_other)(clean_later(h, p).wait_recv)
+            other_pair(h, p).start()
 
     def pass_grads(h):
-        grad_pair(h).wait_recv()
-        later_out[h] = (grad_own[h, 2] + grad_in[h, 2].astype(jnp.float32)).astype(jnp.bfloat16)
-        pl.when(has_other)(grad_later(h).start)
+        for p in range(2):
+            grad_other(h, p).wait_recv()
+            later_out[h, p] = (grad_own[h, 2, p] + grad_in[h, 2, p].astype(jnp.float32)).astype(
+                jnp.bfloat16
+            )
+            pl.when(has_other)(grad_later(h, p).start)
+        for p in range(2):
+            grad_prev(h, p).wait_recv()
+            grad_own[h, 1, p] = grad_own[h, 1, p] + grad_in[h, 1, p].astype(jnp.float32)
         cols = pl.ds(pl.multiple_of(h * HEAD_SIZE, HEAD_SIZE), HEAD_SIZE)
-        total = grad_own[h, 0] + grad_in[h, 0].astype(jnp.float32)
-        scaled = total[0, :rows] * key_gain[cols].reshape(1, HEAD_SIZE)
-        k_scaled[:, cols] = scaled
-        inner[1] += scaled * raw_k[:, cols].astype(jnp.float32)
-        grad_v_ref[:, cols] = total[1, :rows].astype(jnp.bfloat16)
-        grad_own[h, 1] = grad_own[h, 1] + grad_in[h, 1].astype(jnp.float32)
+        for p in range(2):
+            grad_noisy(h, p).wait_recv()
+            total = grad_own[h, 0, p] + grad_in[h, 0, p].astype(jnp.float32)
+            if p == 0:
+                scaled = total[:rows] * key_gain[cols].reshape(1, HEAD_SIZE)
+                k_scaled[:, cols] = scaled
+                inner[1] += scaled * raw_k[:, cols].astype(jnp.float32)
+            else:
+                grad_v_ref[:, cols] = total[:rows].astype(jnp.bfloat16)
 
     def pass_later(h):
-        pl.when(has_later)(grad_later(h).wait_recv)
-        arrived = later_in[h].astype(jnp.float32)
+        for p in range(2):
+            pl.when(has_later)(grad_later(h, p).wait_recv)
+            arrived = later_in[h, p].astype(jnp.float32)
+            own = take_own[...] > 0.0
+            next_out[h, p] = (grad_own[h, 1, p] + jnp.where(own, 0.0, arrived)).astype(
+                jnp.bfloat16
+            )
+            pl.when(has_prev)(grad_next(h, p).start)
+
+    def clean_total(h, p):
+        pl.when(has_next)(grad_next(h, p).wait_recv)
         own = take_own[...] > 0.0
-        next_out[h] = (grad_own[h, 1] + jnp.where(own, 0.0, arrived)).astype(jnp.bfloat16)
-        pl.when(has_prev)(grad_next(h).start)
-
-    def finish(h):
-        pl.when(has_next)(grad_next(h).wait_recv)
-        own = take_own[...] > 0.0
-        total = next_in[h].astype(jnp.float32) + jnp.where(
-            own, later_in[h].astype(jnp.float32), 0.0
-        )
-        cols = pl.ds(pl.multiple_of(h * HEAD_SIZE, HEAD_SIZE), HEAD_SIZE)
-        scaled = total[0, :rows] * key_gain[cols].reshape(1, HEAD_SIZE)
+        arrived = later_in[h, p].astype(jnp.float32)
+        return (next_in[h, p].astype(jnp.float32) + jnp.where(own, arrived, 0.0))[:rows]
+
+    def finish_keys(h):
+        cols = slice(h * HEAD_SIZE, (h + 1) * HEAD_SIZE)
+        scaled = clean_total(h, 0) * key_gain[cols].reshape(1, HEAD_SIZE)
         c_scaled[:, cols] = scaled
         inner[2] += scaled * raw_c[:, cols].astype(jnp.float32)
-        grad_cv_ref[:, cols] = total[1, :rows].astype(jnp.bfloat16)
+
+    def finish_values(h):
+        cols = slice(h * HEAD_SIZE, (h + 1) * HEAD_SIZE)
+        grad_cv_ref[:, cols] = clean_total(h, 1).astype(jnp.bfloat16)
 
     def norm_grad(ref, raw, scaled, at, inner_sum, width):
         inv = inverse_rms[at]
@@ -299,16 +316,17 @@
     for h in range(min(2, heads)):
         pass_clean(h)
         if h + 2 < heads:
-            pl.when(has_next)(value_next(h + 2).start)
-            pl.when(has_next)(key_next(h + 2).start)
+            for p in (1, 0):
+                pl.when(has_next)(clean_next(h + 2, p).start)
     pass_other(0)
 
     own_par = (noisy_own, noisy_par, prev_own, prev_par, other_own, other_par)
 
     def step(h, carry):
-        noisy_pair(h).wait_recv()
-        prev_pair(h).wait_recv()
-        other_pair(h).wait_recv()
+        for p in range(2):
+            noisy_pair(h, p).wait_recv()
+            prev_pair(h, p).wait_recv()
+            other_pair(h, p).wait_recv()
         keys = key_pieces(own_par, h, 0)
         values = key_pieces(own_par, h, 1)
         for member in range(GROUP):
@@ -356,46 +374,50 @@
             )
             return across.T
 
-        dk_total = key_sums(all_queries, all_dscores) * (1.0 / LOG2E)
-        dv_total = key_sums(all_grads, all_weights)
-        for index in range(PIECES // 2):
-            for part, total in enumerate((dk_total, dv_total)):
+        for part in range(2):
+            if part == 0:
+                total = key_sums(all_queries, all_dscores) * (1.0 / LOG2E)
+            else:
+                total = key_sums(all_grads, all_weights)
+            for index in (2, 1, 0):
                 at = 2 * index * piece_rows
-                grad_own[h, index, part] = total[at : at + piece_rows]
                 grad_out[h, index, part] = total[at + piece_rows : at + 2 * piece_rows].astype(
                     jnp.bfloat16
                 )
-        grad_pair(h).start()
+                (grad_noisy, grad_prev, grad_other)[index](h, part).start()
+                grad_own[h, index, part] = total[at : at + piece_rows]
         return carry
 
     lax.fori_loop(0, heads, step, 0)
+    for h in range(max(heads - 2, 0), heads - 1):
+        pass_later(h)
     pass_grads(heads - 1)
     share(1, [jnp.sum(inner[at], axis=1, keepdims=True) for at in range(2)])
-    for h in range(max(heads - 2, 0), heads):
-        pass_later(h)
+    for h in range(heads - 2):
+        finish_keys(h)
+    pass_later(heads - 1)
     totals = shared(1)
     norm_grad(grad_q_ref, raw_q, q_scaled, 0, totals[:, 0:1], q_width)
     norm_grad(grad_k_ref, raw_k, k_scaled, 1, totals[:, 1:2], key_width)
+    for h in range(max(heads - 2, 0), heads):
+        finish_keys(h)
+    share(2, [jnp.sum(inner[2], axis=1, keepdims=True)])
     for h in range(heads):
-        finish(h)
-    share(2, [jnp.sum(inner[2], axis=1, keepdims=True)])
+        finish_values(h)
     totals = shared(2)
     norm_grad(grad_ck_ref, raw_c, c_scaled, 2, totals[:, 0:1], key_width)
-    for h in range(heads):
-        for kind in (noisy_pair, prev_pair, other_pair, grad_pair):
-            kind(h).wait_send()
-
-    def wait_sends(held, kinds):
-        @pl.when(held)
-        def _():
-            for h in range(heads):
-                for kind in kinds:
-                    kind(h).wait_send()
-
-    wait_sends(has_next, (value_next, key_next))
-    wait_sends(has_later, (clean_later,))
-    wait_sends(has_other, (grad_later,))
-    wait_sends(has_prev, (grad_next,))
+
+    def wait_sends(copies):
+        for h in range(heads):
+            for p in range(2):
+                for kind in copies:
+                    kind(h, p).wait_send()
+
+    wait_sends((noisy_pair, prev_pair, other_pair, grad_noisy, grad_prev, grad_other))
+    pl.when(has_next)(lambda: wait_sends((clean_next,)))
+    pl.when(has_later)(lambda: wait_sends((clean_later,)))
+    pl.when(has_other)(lambda: wait_sends((grad_later,)))
+    pl.when(has_prev)(lambda: wait_sends((grad_next,)))
     for kind in range(3):
         for step_by in range(1, sides):
             stat_copy(kind, step_by).wait_send()
@@ -458,8 +480,8 @@
             pltpu.VMEM((stacked[0], HEAD_SIZE), jnp.bfloat16),
             pltpu.VMEM((3, piece_rows, HEAD_SIZE), jnp.float32),
             pltpu.VMEM((3, max(sides - 1, 1), piece_rows, HEAD_SIZE), jnp.float32),
-            pltpu.SemaphoreType.DMA((9, heads)),
-            pltpu.SemaphoreType.DMA((9, heads)),
+            pltpu.SemaphoreType.DMA((10, heads, 2)),
+            pltpu.SemaphoreType.DMA((10, heads, 2)),
             pltpu.SemaphoreType.DMA((3, max(sides - 1, 1))),
             pltpu.SemaphoreType.DMA((3, max(sides - 1, 1))),
         ],
@@ -472,15 +494,12 @@
             transcendentals=rows * GROUP * heads * key_rows,
         ),
     )(*args)
-    blocks = [
-        pl.BlockSpec((rows, array.shape[1] // heads), lambda j: (0, j)) for array in results
-    ]
     return pl.pallas_call(
         hand_over_kernel,
-        grid=(heads,),
-        in_specs=blocks,
-        out_specs=blocks,
+        in_specs=[vmem] * 6,
+        out_specs=[vmem] * 6,
         out_shape=[wide, wide, narrow, narrow, narrow, narrow],
+        compiler_params=pltpu.CompilerParams(vmem_limit_bytes=32 * 1024 * 1024),
     )(*results)
 
 

time: 77.2 us -> 78.1 us (1.012)
  local copies, waits for them, and re-layouts: 1.35 us -> 7.43 us
  Pallas kernels: 75 us -> 69.6 us
    unnamed x1 -> x13, local copies, waits for them, and re-layouts: 1.35 us -> 7.43 us
    pallas_call x1, Pallas kernels: 70.9 us -> 67.9 us  [on_device(): pl.pallas_call(stretch_kernel, in_specs=[pl.BlockSpec(memory_space=pltpu....]
    pallas_call x1, Pallas kernels: 4.11 us -> 1.68 us  [on_device(): pl.pallas_call(hand_over_kernel, in_specs=[vmem] * 6, out_specs=[vmem] *...]
where the time goes in v6:
time: 78.1 us; the launch traced here: 77.7 us
  Pallas kernels  69.6 us (89%)
  local copies, waits for them, and re-layouts  7.43 us (10%)
    pallas_call x1, Pallas kernels, on_device(): pl.pallas_call(stretch_kernel, in_specs=[pl.BlockSpec(memory_space=pltpu....  67.9 us
    unnamed x13, local copies, waits for them, and re-layouts  7.43 us
    pallas_call x1, Pallas kernels, on_device(): pl.pallas_call(hand_over_kernel, in_specs=[vmem] * 6, out_specs=[vmem] *...  1.68 us

profile of v6, /device:TPU:0, one launch (start us, length us, event | category | flops | bytes accessed | tf_op | source)
XLA Modules:
  0.0 77.7 jit_solution(6546113669251849539)
XLA Ops:
  0.6 1.3 %copy.15.window = s32[8,2]{1,0:T(8,128)} copy(s32[8,2]{0,1:T(2,128)} %param.17) | data formatting | bytes 128 | tf_op args[8]
  2.0 67.9 %shard_map.136 = (bf16[260,1536]{1,0:T(8,128)(2,1)}, bf16[260,1536]{1,0:T(8,128)(2,1)}, bf16[260,512]{1,0:T(8,128)(2,1)}, bf16[260,512]{1,0:T(8,128)(2,1)}, bf16...) custom-call(s32[8,2]{1,0:T(8,128)} %copy.15.window, bf16[260,1536]{1,0:T(8,128)(2,1)} %raw_q.1, bf16[260,512]{1,0:T(8,128)(2,1)} %raw_k.1, ...), custom_call_target="tpu_custom_call" | custom-call | flops 7821066240 | bytes 16777216 | tf_op jit(solution)/shard_map/pallas_call | solution.py:457
  69.9 0.0 copy-start
  69.9 1.1 %copy-done = bf16[260,1536]{1,0:T(8,128)(2,1)S(1)} copy-done((bf16[260,1536]{1,0:T(8,128)(2,1)S(1)}, bf16[260,1536]{1,0:T(8,128)(2,1)}, u32[]{:S(2)}) %copy-start) | copy-done | bytes 798744
  71.1 0.0 copy-start.1
  71.1 1.1 %copy-done.1 = bf16[260,1536]{1,0:T(8,128)(2,1)S(1)} copy-done((bf16[260,1536]{1,0:T(8,128)(2,1)S(1)}, bf16[260,1536]{1,0:T(8,128)(2,1)}, u32[]{:S(2)}) %copy-start.1) | copy-done | bytes 798744
  72.2 0.0 copy-start.2
  72.2 1.0 %copy-done.2 = bf16[260,512]{1,0:T(8,128)(2,1)S(1)} copy-done((bf16[260,512]{1,0:T(8,128)(2,1)S(1)}, bf16[260,512]{1,0:T(8,128)(2,1)}, u32[]{:S(2)}) %copy-start.2) | copy-done | bytes 266264
  73.2 0.0 copy-start.3
  73.2 1.0 %copy-done.3 = bf16[260,512]{1,0:T(8,128)(2,1)S(1)} copy-done((bf16[260,512]{1,0:T(8,128)(2,1)S(1)}, bf16[260,512]{1,0:T(8,128)(2,1)}, u32[]{:S(2)}) %copy-start.3) | copy-done | bytes 266264
  74.1 0.0 copy-start.4
  74.1 1.0 %copy-done.4 = bf16[260,512]{1,0:T(8,128)(2,1)S(1)} copy-done((bf16[260,512]{1,0:T(8,128)(2,1)S(1)}, bf16[260,512]{1,0:T(8,128)(2,1)}, u32[]{:S(2)}) %copy-start.4) | copy-done | bytes 266264
  75.1 0.0 copy-start.5
  75.1 1.0 %copy-done.5 = bf16[260,512]{1,0:T(8,128)(2,1)S(1)} copy-done((bf16[260,512]{1,0:T(8,128)(2,1)S(1)}, bf16[260,512]{1,0:T(8,128)(2,1)}, u32[]{:S(2)}) %copy-start.5) | copy-done | bytes 266264
  76.0 1.7 %shard_map.137 = (bf16[260,1536]{1,0:T(8,128)(2,1)}, bf16[260,1536]{1,0:T(8,128)(2,1)}, bf16[260,512]{1,0:T(8,128)(2,1)}, bf16[260,512]{1,0:T(8,128)(2,1)}, bf16...) custom-call(bf16[260,1536]{1,0:T(8,128)(2,1)S(1)} %copy-done, bf16[260,1536]{1,0:T(8,128)(2,1)S(1)} %copy-done.1, ...), custom_call_target="tpu_custom_call" | custom-call | tf_op jit(solution)/shard_map/pallas_call | solution.py:497
Async XLA Ops:
  69.9 1.1 %copy-start = (bf16[260,1536]{1,0:T(8,128)(2,1)S(1)}, bf16[260,1536]{1,0:T(8,128)(2,1)}, u32[]{:S(2)}) copy-start(bf16[260,1536]{1,0:T(8,128)(2,1)} %get-tuple-element.12.refs_0_) | copy-start | bytes 2396164
  71.1 1.1 %copy-start.1 = (bf16[260,1536]{1,0:T(8,128)(2,1)S(1)}, bf16[260,1536]{1,0:T(8,128)(2,1)}, u32[]{:S(2)}) copy-start(bf16[260,1536]{1,0:T(8,128)(2,1)} %get-tuple-element.13.refs_1_) | copy-start | bytes 2396164
  72.2 1.0 %copy-start.2 = (bf16[260,512]{1,0:T(8,128)(2,1)S(1)}, bf16[260,512]{1,0:T(8,128)(2,1)}, u32[]{:S(2)}) copy-start(bf16[260,512]{1,0:T(8,128)(2,1)} %get-tuple-element.14.refs_2_) | copy-start | bytes 798724
  73.2 1.0 %copy-start.3 = (bf16[260,512]{1,0:T(8,128)(2,1)S(1)}, bf16[260,512]{1,0:T(8,128)(2,1)}, u32[]{:S(2)}) copy-start(bf16[260,512]{1,0:T(8,128)(2,1)} %get-tuple-element.15.refs_3_) | copy-start | bytes 798724
  74.1 1.0 %copy-start.4 = (bf16[260,512]{1,0:T(8,128)(2,1)S(1)}, bf16[260,512]{1,0:T(8,128)(2,1)}, u32[]{:S(2)}) copy-start(bf16[260,512]{1,0:T(8,128)(2,1)} %get-tuple-element.16.refs_4_) | copy-start | bytes 798724
  75.1 1.0 %copy-start.5 = (bf16[260,512]{1,0:T(8,128)(2,1)S(1)}, bf16[260,512]{1,0:T(8,128)(2,1)}, u32[]{:S(2)}) copy-start(bf16[260,512]{1,0:T(8,128)(2,1)} %get-tuple-element.17.refs_5_) | copy-start | bytes 798724

commit v7 on v6

--- a/solution.py
+++ b/solution.py
@@ -494,12 +494,17 @@
             transcendentals=rows * GROUP * heads * key_rows,
         ),
     )(*args)
+    parts = 2 if heads % 2 == 0 else 1
+    blocks = [
+        pl.BlockSpec((rows, array.shape[1] // parts), lambda j: (0, j)) for array in results
+    ]
     return pl.pallas_call(
         hand_over_kernel,
-        in_specs=[vmem] * 6,
-        out_specs=[vmem] * 6,
+        grid=(parts,),
+        in_specs=blocks,
+        out_specs=blocks,
         out_shape=[wide, wide, narrow, narrow, narrow, narrow],
-        compiler_params=pltpu.CompilerParams(vmem_limit_bytes=32 * 1024 * 1024),
+        compiler_params=pltpu.CompilerParams(vmem_limit_bytes=58 * 1024 * 1024),
     )(*results)
 
 

time: 78.1 us -> 73 us (0.935)
  local copies, waits for them, and re-layouts: 7.43 us -> 1.35 us
  Pallas kernels: 69.6 us -> 70.8 us
    unnamed x13 -> x1, local copies, waits for them, and re-layouts: 7.43 us -> 1.35 us
    pallas_call x1, Pallas kernels: 1.68 us -> 2.92 us  [on_device(): pl.pallas_call(hand_over_kernel, grid=(parts,), in_specs=blocks, out_spec...]
where the time goes in v7:
time: 73 us; the launch traced here: 72.8 us
  Pallas kernels  70.8 us (97%)
  local copies, waits for them, and re-layouts  1.35 us (2%)
    pallas_call x1, Pallas kernels, on_device(): pl.pallas_call(stretch_kernel, in_specs=[pl.BlockSpec(memory_space=pltpu....  67.9 us
    pallas_call x1, Pallas kernels, on_device(): pl.pallas_call(hand_over_kernel, grid=(parts,), in_specs=blocks, out_spec...  2.92 us

profile of v7, /device:TPU:0, one launch (start us, length us, event | category | flops | bytes accessed | tf_op | source)
XLA Modules:
  0.0 72.8 jit_solution(3749607680379505359)
XLA Ops:
  0.6 1.3 %copy.15.window = s32[8,2]{1,0:T(8,128)} copy(s32[8,2]{0,1:T(2,128)} %param.17) | data formatting | bytes 128 | tf_op args[8]
  2.0 67.9 %shard_map.136 = (bf16[260,1536]{1,0:T(8,128)(2,1)}, bf16[260,1536]{1,0:T(8,128)(2,1)}, bf16[260,512]{1,0:T(8,128)(2,1)}, bf16[260,512]{1,0:T(8,128)(2,1)}, bf16...) custom-call(s32[8,2]{1,0:T(8,128)} %copy.15.window, bf16[260,1536]{1,0:T(8,128)(2,1)} %raw_q.1, bf16[260,512]{1,0:T(8,128)(2,1)} %raw_k.1, ...), custom_call_target="tpu_custom_call" | custom-call | flops 7821066240 | bytes 16777216 | tf_op jit(solution)/shard_map/pallas_call | solution.py:457
  69.9 2.9 %shard_map.137 = (bf16[260,1536]{1,0:T(8,128)(2,1)}, bf16[260,1536]{1,0:T(8,128)(2,1)}, bf16[260,512]{1,0:T(8,128)(2,1)}, bf16[260,512]{1,0:T(8,128)(2,1)}, bf16...) custom-call(bf16[260,1536]{1,0:T(8,128)(2,1)} %get-tuple-element.12.refs_0_, bf16[260,1536]{1,0:T(8,128)(2,1)} %get-tuple-element.13.refs_1_, ...), custom_call_target="tpu_custom_call" | custom-call | tf_op jit(solution)/shard_map/pallas_call | solution.py:501
